TPU v7x, 128 devices: a whole 4x4x4 slice. The times are simulated.
128 devices in a mesh: slab: 4 (over x), pen: 32 (over z, y, core).
Axes of the slice: x: 4, y: 4, z: 4, core: 2. Of those that a mesh axis runs over, the one named last changes fastest.
Arguments:
- volume: bfloat16 [256, 128, 64, 128], P(None, 'pen', 'slab'), may hold values from -6 to 6
- occupancy: int32 [16, 8, 4], replicated, may hold values from 0 to 1, as said below
- gains: float32 [3, 128], replicated, may hold values from 0.5 to 1.5
- w_query: bfloat16 [3, 128, 128], replicated, as said below
- w_key: bfloat16 [3, 128, 128], replicated, as said below
- w_value: bfloat16 [3, 128, 128], replicated, may hold values from -0.5 to 0.5
- w_out: bfloat16 [3, 128, 128], replicated, may hold values from -0.5 to 0.5
Outputs:
- result: bfloat16 [256, 128, 64, 128], P(None, 'pen', 'slab')
Inputs may be any that keep to these rules, and one draw needn't show every extreme that they name: `occupancy`: entries are 0 or 1; for every y-tile and z-tile index, each aligned group of 4 consecutive x-tiles holds exactly one occupied tile. `w_query`: entries lie within -24 / sqrt(128) and 24 / sqrt(128). `w_key`: entries lie within -24 / sqrt(128) and 24 / sqrt(128).
All inputs are finite; a program needn't handle non-finite values.
Results may differ from a plain program's by a relative error of at most 0.015.
Values may be sent and summed in bfloat16 or wider, within the bound.
No kernel may reach another device: no remote copies, remote signals or barrier semaphores. Data moves between devices by JAX's collectives and lax.ppermute only.
A program may use at most 128 MiB of HBM per device.

v0:
```python
import math

import jax
import jax.numpy as jnp
from jax import lax
from jax.sharding import PartitionSpec as P

HEADS = 8
TILE = 16


def tile_lookup(occupancy, index_x, index_y, index_z):
    picked = jnp.take(occupancy, index_x // TILE, axis=0)
    picked = jnp.take(picked, index_y // TILE, axis=1)
    return jnp.take(picked, index_z // TILE, axis=2)


def span(start, count):
    return start + jnp.arange(count)


def block_attend(rows_in, alive_mask, gain, w_query, w_key, w_value, w_out):
    count_lines, length, width = rows_in.shape
    head_size = width // HEADS
    widened = rows_in.astype(jnp.float32)
    row_mean = jnp.mean(widened, axis=-1, keepdims=True)
    centred = widened - row_mean
    row_var = jnp.mean(centred * centred, axis=-1, keepdims=True)
    normed = (centred * lax.rsqrt(row_var + 1e-05) * gain).astype(jnp.bfloat16)
    flat_rows = normed.reshape(count_lines * length, width)
    shaped = (count_lines, length, HEADS, head_size)
    query_rows = (
        jnp.dot(flat_rows, w_query, preferred_element_type=jnp.float32)
        .astype(jnp.bfloat16)
        .reshape(shaped)
    )
    key_rows = (
        jnp.dot(flat_rows, w_key, preferred_element_type=jnp.float32)
        .astype(jnp.bfloat16)
        .reshape(shaped)
    )
    value_rows = (
        jnp.dot(flat_rows, w_value, preferred_element_type=jnp.float32)
        .astype(jnp.bfloat16)
        .reshape(shaped)
    )
    scores = jnp.einsum(
        "blhe,bmhe->bhlm", query_rows, key_rows, preferred_element_type=jnp.float32
    ) * (1.0 / math.sqrt(head_size))
    live_keys = alive_mask[:, None, None, :] > 0
    scores = jnp.where(live_keys, scores, -1e30)
    row_top = jnp.max(scores, axis=-1, keepdims=True)
    exponent = jnp.exp(scores - row_top)
    row_total = jnp.sum(exponent, axis=-1, keepdims=True)
    weights = (exponent / row_total).astype(jnp.bfloat16)
    attended = jnp.einsum(
        "bhlm,bmhe->blhe", weights, value_rows, preferred_element_type=jnp.float32
    ).astype(jnp.bfloat16)
    update = jnp.dot(
        attended.reshape(count_lines * length, width), w_out, preferred_element_type=jnp.float32
    ).reshape(count_lines, length, width)
    update = jnp.where(alive_mask[:, :, None] > 0, update, 0.0)
    return (widened + update).astype(jnp.bfloat16)


def along_axis(volume, alive, axis, params):
    moved = jnp.moveaxis(volume, axis, -2)
    alive_moved = jnp.moveaxis(alive, axis, -1)
    length = moved.shape[-2]
    width = moved.shape[-1]
    line_count = moved.shape[0] * moved.shape[1]
    per_block = min(line_count, max(1, 2048 // length))
    grouped = moved.reshape(line_count // per_block, per_block, length, width)
    alive_grouped = alive_moved.reshape(line_count // per_block, per_block, length)

    def apply_block(packed):
        return block_attend(packed[0], packed[1], *params)

    result = lax.map(apply_block, (grouped, alive_grouped))
    result = result.reshape(moved.shape)
    return jnp.moveaxis(result, -2, axis)


def body(volume, occupancy, gains, w_query, w_key, w_value, w_out):
    pen_pos = lax.axis_index("pen")
    slab_pos = lax.axis_index("slab")
    pen_count = lax.axis_size("pen")
    slab_count = lax.axis_size("slab")
    full_x, plane_y, plane_z, width = volume.shape
    own_x = full_x // pen_count
    full_y = plane_y * pen_count
    full_z = plane_z * slab_count

    def phase_params(phase):
        return (gains[phase], w_query[phase], w_key[phase], w_value[phase], w_out[phase])

    alive = tile_lookup(
        occupancy,
        span(0, full_x),
        span(pen_pos * plane_y, plane_y),
        span(slab_pos * plane_z, plane_z),
    )
    section_x = along_axis(volume, alive, 0, phase_params(0))
    owned_x = span(pen_pos * own_x, own_x)
    across_y = lax.all_to_all(section_x, "pen", split_axis=0, concat_axis=1, tiled=True)
    alive = tile_lookup(occupancy, owned_x, span(0, full_y), span(slab_pos * plane_z, plane_z))
    section_y = along_axis(across_y, alive, 1, phase_params(1))
    across_z = lax.all_to_all(section_y, "slab", split_axis=1, concat_axis=2, tiled=True)
    part_y = full_y // slab_count
    alive = tile_lookup(occupancy, owned_x, span(slab_pos * part_y, part_y), span(0, full_z))
    section_z = along_axis(across_z, alive, 2, phase_params(2))
    back_rows = lax.all_to_all(section_z, "slab", split_axis=2, concat_axis=1, tiled=True)
    return lax.all_to_all(back_rows, "pen", split_axis=1, concat_axis=0, tiled=True)


def solution(mesh):
    placed = (P(None, "pen", "slab", None), P(), P(), P(), P(), P(), P())
    return jax.shard_map(
        body, mesh=mesh, in_specs=placed, out_specs=P(None, "pen", "slab", None), check_vma=False
    )
```

profile of v0, /device:TPU:1, one launch (start us, length us, event | category | flops | bytes accessed | tf_op | source)
XLA Modules:
  0.0 791.3 jit_solution(11443373032570204033)
XLA Ops:
  13.4 205.4 %while.30 = (s32[]{:T(128)}, bf16[8,8,256,128]{3,1,0,2:T(8,128)(2,1)}, bf16[8,8,256,128]{3,2,1,0:T(8,128)(2,1)}, s32[8,8,256]{2,1,0:T(8,128)S(1)}, f32[1,128]{1,...) while((s32[]{:T(128)}, ...), condition=%wide.region_5.6_spmd, body=%wide.region_0.5_spmd.sunk | while | flops 567021824 | bytes 50199672 | solution.py:79
  19.6 9.4 %fusion.204 = (f32[8,8,256]{2,1,0:T(8,128)S(1)}, f32[8,8,256,256]{2,3,1,0:T(8,128)}) fusion(pred[8,256]{1,0:T(8,128)(4,1)S(1)} %fusion.200, bf16[8,256,8,16]{1,0,3,2:T(8,128)(2,1)S(1)} %bitcast.360, bf16[8,256,8,16]{1,0,3,2:T(8,128)(2,1)S(1)} %bitcast.362), kind=kOutput, calls=%fused_computation.232.clone.1 | convolution fusion | flops 150995200 | bytes 17893376 | tf_op jit(solution)/shard_map/while/body/eval_jaxpr/sub | solution.py:53
  29.7 7.0 fusion.205
  45.2 9.4 %fusion.204 = (f32[8,8,256]{2,1,0:T(8,128)S(1)}, f32[8,8,256,256]{2,3,1,0:T(8,128)}) fusion(pred[8,256]{1,0:T(8,128)(4,1)S(1)} %fusion.200, bf16[8,256,8,16]{1,0,3,2:T(8,128)(2,1)S(1)} %bitcast.360, bf16[8,256,8,16]{1,0,3,2:T(8,128)(2,1)S(1)} %bitcast.362), kind=kOutput, calls=%fused_computation.232.clone.1 | convolution fusion | flops 150995200 | bytes 17893376 | tf_op jit(solution)/shard_map/while/body/eval_jaxpr/sub | solution.py:53
  55.3 7.0 fusion.205
  70.9 9.4 %fusion.204 = (f32[8,8,256]{2,1,0:T(8,128)S(1)}, f32[8,8,256,256]{2,3,1,0:T(8,128)}) fusion(pred[8,256]{1,0:T(8,128)(4,1)S(1)} %fusion.200, bf16[8,256,8,16]{1,0,3,2:T(8,128)(2,1)S(1)} %bitcast.360, bf16[8,256,8,16]{1,0,3,2:T(8,128)(2,1)S(1)} %bitcast.362), kind=kOutput, calls=%fused_computation.232.clone.1 | convolution fusion | flops 150995200 | bytes 17893376 | tf_op jit(solution)/shard_map/while/body/eval_jaxpr/sub | solution.py:53
  80.9 7.0 fusion.205
  96.5 9.4 %fusion.204 = (f32[8,8,256]{2,1,0:T(8,128)S(1)}, f32[8,8,256,256]{2,3,1,0:T(8,128)}) fusion(pred[8,256]{1,0:T(8,128)(4,1)S(1)} %fusion.200, bf16[8,256,8,16]{1,0,3,2:T(8,128)(2,1)S(1)} %bitcast.360, bf16[8,256,8,16]{1,0,3,2:T(8,128)(2,1)S(1)} %bitcast.362), kind=kOutput, calls=%fused_computation.232.clone.1 | convolution fusion | flops 150995200 | bytes 17893376 | tf_op jit(solution)/shard_map/while/body/eval_jaxpr/sub | solution.py:53
  106.6 7.0 fusion.205
  122.1 9.4 %fusion.204 = (f32[8,8,256]{2,1,0:T(8,128)S(1)}, f32[8,8,256,256]{2,3,1,0:T(8,128)}) fusion(pred[8,256]{1,0:T(8,128)(4,1)S(1)} %fusion.200, bf16[8,256,8,16]{1,0,3,2:T(8,128)(2,1)S(1)} %bitcast.360, bf16[8,256,8,16]{1,0,3,2:T(8,128)(2,1)S(1)} %bitcast.362), kind=kOutput, calls=%fused_computation.232.clone.1 | convolution fusion | flops 150995200 | bytes 17893376 | tf_op jit(solution)/shard_map/while/body/eval_jaxpr/sub | solution.py:53
  132.2 7.0 fusion.205
  147.8 9.4 %fusion.204 = (f32[8,8,256]{2,1,0:T(8,128)S(1)}, f32[8,8,256,256]{2,3,1,0:T(8,128)}) fusion(pred[8,256]{1,0:T(8,128)(4,1)S(1)} %fusion.200, bf16[8,256,8,16]{1,0,3,2:T(8,128)(2,1)S(1)} %bitcast.360, bf16[8,256,8,16]{1,0,3,2:T(8,128)(2,1)S(1)} %bitcast.362), kind=kOutput, calls=%fused_computation.232.clone.1 | convolution fusion | flops 150995200 | bytes 17893376 | tf_op jit(solution)/shard_map/while/body/eval_jaxpr/sub | solution.py:53
  157.8 7.0 fusion.205
  173.4 9.4 %fusion.204 = (f32[8,8,256]{2,1,0:T(8,128)S(1)}, f32[8,8,256,256]{2,3,1,0:T(8,128)}) fusion(pred[8,256]{1,0:T(8,128)(4,1)S(1)} %fusion.200, bf16[8,256,8,16]{1,0,3,2:T(8,128)(2,1)S(1)} %bitcast.360, bf16[8,256,8,16]{1,0,3,2:T(8,128)(2,1)S(1)} %bitcast.362), kind=kOutput, calls=%fused_computation.232.clone.1 | convolution fusion | flops 150995200 | bytes 17893376 | tf_op jit(solution)/shard_map/while/body/eval_jaxpr/sub | solution.py:53
  183.5 7.0 fusion.205
  199.0 9.4 %fusion.204 = (f32[8,8,256]{2,1,0:T(8,128)S(1)}, f32[8,8,256,256]{2,3,1,0:T(8,128)}) fusion(pred[8,256]{1,0:T(8,128)(4,1)S(1)} %fusion.200, bf16[8,256,8,16]{1,0,3,2:T(8,128)(2,1)S(1)} %bitcast.360, bf16[8,256,8,16]{1,0,3,2:T(8,128)(2,1)S(1)} %bitcast.362), kind=kOutput, calls=%fused_computation.232.clone.1 | convolution fusion | flops 150995200 | bytes 17893376 | tf_op jit(solution)/shard_map/while/body/eval_jaxpr/sub | solution.py:53
  209.1 7.0 fusion.205
  218.8 10.4 %all-to-all-start = ((bf16[256,4,16,128]{3,2,1,0:T(8,128)(2,1)}), bf16[256,4,16,128]{3,2,1,0:T(8,128)(2,1)}, u32[]{:S(2)}, u32[]{:S(2)}) async-start(bf16[256,4,16,128]{3,2,1,0:T(8,128)(2,1)} %bitcast.39), calls=%async_computation | async-start | bytes 8388608 | tf_op jit(solution)/shard_map/all_to_all | solution.py:105
  231.7 47.4 %all-to-all-done = bf16[256,4,16,128]{3,2,1,0:T(8,128)(2,1)} async-done(((bf16[256,4,16,128]{3,2,1,0:T(8,128)(2,1)}), bf16[256,4,16,128]{3,2,1,0:T(8,128)(2,1)}, u32[]{:S(2)}, u32[]{:S(2)}) %all-to-all-start) | async-done | bytes 4194336 | tf_op jit(solution)/shard_map/all_to_all | solution.py:105
  284.7 134.5 %while.31 = (s32[]{:T(128)}, bf16[8,16,128,128]{3,1,0,2:T(8,128)(2,1)}, bf16[8,16,128,128]{3,1,2,0:T(8,128)(2,1)}, s32[8,16,128]{2,0,1:T(8,128)S(1)}, f32[1,128]...) while((s32[]{:T(128)}, ...), condition=%wide.region_11.13_spmd, body=%wide.region_6.12_spmd.sunk | while | flops 420221056 | bytes 34454636 | solution.py:79
  426.2 43.5 %all-to-all-done.1 = bf16[8,128,16,128]{3,2,0,1:T(8,128)(2,1)} async-done(((bf16[8,128,16,128]{3,2,0,1:T(8,128)(2,1)}), bf16[8,128,16,128]{3,2,0,1:T(8,128)(2,1)}, u32[]{:S(2)}, u32[]{:S(2)}) %all-to-all-start.1) | async-done | bytes 4194336 | tf_op jit(solution)/shard_map/all_to_all | solution.py:108
  475.2 193.1 %while.32 = (s32[]{:T(128)}, bf16[8,32,64,128]{3,1,0,2:T(8,128)(2,1)}, bf16[8,32,64,128]{3,2,1,0:T(8,128)(2,1)}, s32[8,32,64]{2,1,0:T(8,128)S(1)}, f32[1,128]{1,...) while((s32[]{:T(128)}, ...), condition=%wide.region_17.19_spmd, body=%wide.region_12.18_spmd.sunk | while | flops 348917824 | bytes 33414264 | solution.py:79
  668.3 48.3 %all_to_all.72 = bf16[8,32,64,128]{3,1,0,2:T(8,128)(2,1)S(1)} all-to-all(bf16[8,32,64,128]{3,1,0,2:T(8,128)(2,1)} %get-tuple-element.149), channel_id=1, replica_groups=mesh['slab'=4,'pen'=32] {'slab'}, dimensions={2} | all-to-all | bytes 8388608 | tf_op jit(solution)/shard_map/all_to_all | solution.py:112
  722.7 65.1 %all_to_all.73 = bf16[8,128,16,128]{3,2,0,1:T(8,128)(2,1)S(1)} all-to-all(bf16[8,128,16,128]{3,2,0,1:T(8,128)(2,1)S(1)} %copy.145), channel_id=1, replica_groups=mesh['slab'=4,'pen'=32] {'pen'}, dimensions={1} | all-to-all | bytes 8388608 | tf_op jit(solution)/shard_map/all_to_all | solution.py:113
  (572 shorter events, 441.5 us)
Async XLA Ops:
  0.0 12.1 %copy-start.4 = (bf16[3,128,128]{2,1,0:T(8,128)(2,1)S(1)}, bf16[3,128,128]{2,1,0:T(8,128)(2,1)}, u32[]{:S(2)}) copy-start(bf16[3,128,128]{2,1,0:T(8,128)(2,1)} %param.18) | copy-start | bytes 294916
  0.0 12.1 %copy-start.5 = (bf16[3,128,128]{2,1,0:T(8,128)(2,1)S(1)}, bf16[3,128,128]{2,1,0:T(8,128)(2,1)}, u32[]{:S(2)}) copy-start(bf16[3,128,128]{2,1,0:T(8,128)(2,1)} %param.20) | copy-start | bytes 294916
  0.0 12.8 %copy-start.7 = (bf16[3,128,128]{2,1,0:T(8,128)(2,1)S(1)}, bf16[3,128,128]{2,1,0:T(8,128)(2,1)}, u32[]{:S(2)}) copy-start(bf16[3,128,128]{2,1,0:T(8,128)(2,1)} %param.19) | copy-start | bytes 294916
  0.0 12.8 %copy-start.6 = (bf16[3,128,128]{2,1,0:T(8,128)(2,1)S(1)}, bf16[3,128,128]{2,1,0:T(8,128)(2,1)}, u32[]{:S(2)}) copy-start(bf16[3,128,128]{2,1,0:T(8,128)(2,1)} %param.21) | copy-start | bytes 294916
  218.8 60.4 %all-to-all-start = ((bf16[256,4,16,128]{3,2,1,0:T(8,128)(2,1)}), bf16[256,4,16,128]{3,2,1,0:T(8,128)(2,1)}, u32[]{:S(2)}, u32[]{:S(2)}) async-start(bf16[256,4,16,128]{3,2,1,0:T(8,128)(2,1)} %bitcast.39), calls=%async_computation | async-start | bytes 8388608 | tf_op jit(solution)/shard_map/all_to_all | solution.py:105
  419.2 56.0 %copy-start = (bf16[128,128]{1,0:T(8,128)(2,1)S(1)}, bf16[128,128]{1,0:T(8,128)(2,1)}, u32[]{:S(2)}) copy-start(bf16[128,128]{1,0:T(8,128)(2,1)} %get-tuple-element.542) | copy-start | bytes 98308
  419.2 56.0 %copy-start.1 = (bf16[128,128]{1,0:T(8,128)(2,1)S(1)}, bf16[128,128]{1,0:T(8,128)(2,1)}, u32[]{:S(2)}) copy-start(bf16[128,128]{1,0:T(8,128)(2,1)} %get-tuple-element.540) | copy-start | bytes 98308
  419.2 56.0 %copy-start.2 = (bf16[128,128]{1,0:T(8,128)(2,1)S(1)}, bf16[128,128]{1,0:T(8,128)(2,1)}, u32[]{:S(2)}) copy-start(bf16[128,128]{1,0:T(8,128)(2,1)} %get-tuple-element.539) | copy-start | bytes 98308
  419.2 56.0 %copy-start.3 = (bf16[128,128]{1,0:T(8,128)(2,1)S(1)}, bf16[128,128]{1,0:T(8,128)(2,1)}, u32[]{:S(2)}) copy-start(bf16[128,128]{1,0:T(8,128)(2,1)} %get-tuple-element.541) | copy-start | bytes 98308
  419.2 56.0 %copy-start.8 = (f32[1,128]{1,0:T(1,128)S(1)}, f32[1,128]{1,0:T(1,128)}, u32[]{:S(2)}) copy-start(f32[1,128]{1,0:T(1,128)} %get-tuple-element.538) | copy-start | bytes 1540
  419.2 50.5 %all-to-all-start.1 = ((bf16[8,128,16,128]{3,2,0,1:T(8,128)(2,1)}), bf16[8,128,16,128]{3,2,0,1:T(8,128)(2,1)}, u32[]{:S(2)}, u32[]{:S(2)}) async-start(bf16[8,128,16,128]{3,2,0,1:T(8,128)(2,1)} %bitcast.51), calls=%async_computation.1 | async-start | bytes 8388608 | tf_op jit(solution)/shard_map/all_to_all | solution.py:108
where the time goes:
time: 800 us; the launch traced here: 791 us
  matrix products  313 us (39%)
  other arithmetic  134 us (17%)
  local copies, waits for them, and re-layouts  121 us (15%)
  blocking collectives  113 us (14%)
  waiting for transfers between devices  91 us (11%)
  starting transfers between devices  15.5 us (2%)
    dot_general x24, matrix products, block_attend(): jnp.einsum('bhlm,bmhe->blhe', weights, value_rows, preferred_element_type...  129 us
    sub x16, matrix products, block_attend(): exponent = jnp.exp(scores - row_top)  121 us
    all_to_all x1, blocking collectives, body(): lax.all_to_all(back_rows, 'pen', split_axis=1, concat_axis=0, tiled=True)  65.1 us
    all_to_all x1, blocking collectives, body(): lax.all_to_all(section_z, 'slab', split_axis=2, concat_axis=1, tiled=True)  48.3 us
    all_to_all x1, waiting for transfers between devices, body(): lax.all_to_all(section_x, 'pen', split_axis=0, concat_axis=1, tiled=True)  47.4 us
    sub x8, other arithmetic, block_attend(): exponent = jnp.exp(scores - row_top)  43.9 us
    all_to_all x1, waiting for transfers between devices, body(): lax.all_to_all(section_y, 'slab', split_axis=1, concat_axis=2, tiled=True)  43.5 us
    convert_element_type x24, other arithmetic, block_attend(): normed = (centred * lax.rsqrt(row_var + 1e-05) * gain).astype(jnp.bfloat16)  32.1 us
  transfers between devices with their start and end apart: 2, of which 2 were waited for; matrix products, arithmetic and copies ran while one was open for 1% of the time, Pallas kernels for 0%

commit v1 on v0

v1 whole, which is shorter than its diff:
```python
import functools
import math

import jax
import jax.numpy as jnp
from jax import lax
from jax.experimental import pallas as pl
from jax.experimental.pallas import tpu as pltpu
from jax.sharding import PartitionSpec as P

HEADS = 8
TILE = 16
GROUP = 4
BF16 = jnp.bfloat16
F32 = jnp.float32
BIG = 1e30
XU = 4
ZTS = 2
YTS = 2
GAP = 1
YIELD_AT = (1,3)
VMEM_BYTES = 48 * 2**20


def normalise(rows, gain):
    mean = jnp.mean(rows, axis=-1, keepdims=True)
    centred = rows - mean
    var = jnp.mean(centred * centred, axis=-1, keepdims=True)
    return (centred * lax.rsqrt(var + 1e-05) * gain).astype(BF16)


def dot_nt(a, b):
    return lax.dot_general(a, b, (((1,), (1,)), ((), ())), preferred_element_type=F32)


def dot_tn(a, b):
    return lax.dot_general(a, b, (((0,), (0,)), ((), ())), preferred_element_type=F32)


def dot_nn(a, b):
    return jnp.dot(a, b, preferred_element_type=F32)


def lane_of(width):
    return lax.broadcasted_iota(jnp.int32, (1, width), 1)


def ones_where(condition):
    return jnp.where(condition, 1.0, 0.0).astype(BF16)


def paired(weight):
    low = lane_of(128) < 64
    wide = weight.astype(F32)
    lo, hi = jnp.where(low, wide, 0.0), jnp.where(low, 0.0, wide)
    first = jnp.concatenate([lo, pltpu.roll(hi, 64, 1)], axis=1)
    second = jnp.concatenate([pltpu.roll(lo, 64, 1), hi], axis=1)
    return jnp.concatenate([first, second], axis=0).astype(BF16)


def placed(block, j, low):
    tile = block[:, (j // 2) * 128 : (j // 2 + 1) * 128] * low[j % 2]
    rest = jnp.zeros_like(tile)
    return jnp.concatenate([tile, rest] if j < 2 else [rest, tile], axis=1)


class Weights:
    def __init__(self, phase, gain_ref, w_query_ref, w_key_ref, w_value_ref, w_out_ref):
        self.gain = gain_ref[phase : phase + 1, :]
        self.query = paired(w_query_ref[phase])
        self.key = paired(w_key_ref[phase])
        self.value_t = w_value_ref[phase].astype(F32).T.astype(BF16)
        self.out = w_out_ref[phase]


def staggered(quads):
    results = [None] * len(quads)
    active, turn, started = [], 0, 0
    while active or started < len(quads):
        if started < len(quads) and turn % GAP == 0:
            active.append(started)
            started += 1
        for which in list(active):
            try:
                next(quads[which])
            except StopIteration as stop:
                results[which] = stop.value
                active.remove(which)
        turn += 1
    return sum(results, [])


def attend_quad(lines, weights, mask=None):
    length, width = lines[0].shape
    head_size = width // HEADS
    per_tile = 256 // length
    normed = normalise(jnp.concatenate(lines, axis=0), weights.gain)
    yield
    part = [normed[j * length : (j + 1) * length] for j in range(4)]
    beside = jnp.concatenate(
        [jnp.concatenate(part[0:2], axis=1), jnp.concatenate(part[2:4], axis=1)], axis=0
    )
    query = dot_nn(beside, weights.query).astype(BF16)
    key = dot_nn(beside, weights.key).astype(BF16)
    value_t = dot_nt(weights.value_t, normed).astype(BF16)
    yield
    lane = lane_of(256)
    halves = [ones_where(lane_of(128) // 64 == j) for j in range(2)]
    swap = (lane // 64) % 2 if length == 64 else 0
    head_masks = [ones_where((lane % 64) // head_size == (swap ^ i)) for i in range(4)]
    low = lane_of(128) < 64
    attended = [[] for _ in range(4)]

    def scores_of(half, t):
        lanes = slice(half * 128, (half + 1) * 128)
        query_half = jnp.concatenate([query[:length, lanes], query[length:, lanes]], axis=1)
        key_half = jnp.concatenate([key[:length, lanes], key[length:, lanes]], axis=1)
        key_rows = jnp.concatenate([placed(key_half, j, halves) for j in range(4)], axis=0)
        spread = jnp.concatenate(
            [query_half * head_masks[t * per_tile + i] for i in range(per_tile)], axis=0
        )
        return dot_nt(key_rows, spread)

    def weights_of(line):
        if mask is not None:
            line = line + mask
        top = jnp.max(line, axis=0, keepdims=True)
        line = jnp.exp2((line - top) * (math.log2(math.e) / math.sqrt(head_size)))
        return (line * (1.0 / jnp.sum(line, axis=0, keepdims=True))).astype(BF16)

    def gather(half, t, probs):
        if length == 64:
            values = value_t[half * 64 : (half + 1) * 64]
            lhs = jnp.concatenate([placed(values, j, halves) for j in range(4)], axis=0)
            out = dot_nn(lhs, jnp.concatenate(probs, axis=0))
            for i in range(4):
                at = slice((i // 2) * 128, (i // 2 + 1) * 128)
                for pair in range(2):
                    a = out[pair * 128 + i * 16 : pair * 128 + (i + 1) * 16, at]
                    b = out[pair * 128 + 64 + i * 16 : pair * 128 + 64 + (i + 1) * 16, at]
                    if i % 2:
                        attended[pair].append(pltpu.roll(jnp.where(low, b, a), 64, 1))
                    else:
                        attended[pair].append(jnp.where(low, a, b))
            return
        for pair in range(2):
            rows = slice(half * 64 + t * 32, half * 64 + (t + 1) * 32)
            values = value_t[rows, pair * 256 : (pair + 1) * 256]
            rest = jnp.zeros_like(values[:, :128])
            lhs = jnp.concatenate(
                [
                    jnp.concatenate([values[:, :128], rest], axis=1),
                    jnp.concatenate([rest, values[:, 128:]], axis=1),
                ],
                axis=0,
            )
            out = dot_nn(lhs, jnp.concatenate(probs[pair * 2 : pair * 2 + 2], axis=0))
            for j in range(2):
                for i in range(2):
                    attended[pair * 2 + j].append(
                        out[j * 32 + i * 16 : j * 32 + (i + 1) * 16, i * 128 : (i + 1) * 128]
                    )

    steps = [(half, t) for half in range(2) for t in range(4 // per_tile)]
    scores = scores_of(*steps[0])
    for k, step in enumerate(steps):
        yield
        ahead = scores_of(*steps[k + 1]) if k + 1 < len(steps) else None
        probs = []
        for j in range(4):
            probs.append(weights_of(scores[j * length : (j + 1) * length]))
            if j in YIELD_AT:
                yield
        gather(*step, probs)
        scores = ahead
    yield
    if length == 64:
        new = []
        for pair in range(2):
            joined = jnp.concatenate(attended[pair], axis=0).astype(BF16)
            update = dot_tn(joined, weights.out)
            new += [lines[pair * 2] + update[:64], lines[pair * 2 + 1] + update[64:]]
        return new
    return [
        lines[j] + dot_tn(jnp.concatenate(attended[j], axis=0).astype(BF16), weights.out)
        for j in range(4)
    ]


def label_of(occ_ref, group, tile_y, tile_z):
    label = jnp.int32(0)
    for k in range(1, GROUP):
        label = label + k * occ_ref[tile_y, tile_z, group * GROUP + k]
    return label


def x_kernel(occ_ref, vol_ref, *refs):
    given, (out_ref, res_ref, vin, whole, hs, sems, whole_sems) = refs[:5], refs[5:12]
    weight_refs, weight_sems = refs[12:17], refs[17]
    pen, slab = lax.axis_index("pen"), lax.axis_index("slab")
    tile_y = pen // 4
    loads = []
    for pair in range(2):
        for g in range(4):
            start = (g * GROUP + label_of(occ_ref, g, tile_y, slab)) * TILE
            loads.append(
                pltpu.make_async_copy(
                    vol_ref.at[pl.ds(start, TILE), pl.ds(pair * 2, 2)],
                    vin.at[pair, pl.ds(g * TILE, TILE)],
                    sems.at[pair, g],
                )
            )
            loads[-1].start()
        if pair == 0:
            for k in range(5):
                loads.append(pltpu.make_async_copy(given[k], weight_refs[k], weight_sems.at[k]))
                loads[-1].start()
    fetch = pltpu.make_async_copy(vol_ref, whole, whole_sems.at[0])
    store = pltpu.make_async_copy(whole, res_ref, whole_sems.at[1])
    fetch.start()
    for copy in loads:
        copy.wait()
    weights = Weights(0, *weight_refs)

    def pair_step(pair, carry):
        hs[...] = vin[pair].astype(F32).reshape(64 * 32, 128)

        def step(i, inner):
            at = i * (4 * XU)
            lines = [hs[pl.ds(at + j, 64, stride=32), :] for j in range(4 * XU)]
            new = staggered([attend_quad(lines[4 * u : 4 * u + 4], weights) for u in range(XU)])
            for j in range(4 * XU):
                hs[pl.ds(at + j, 64, stride=32), :] = new[j]
            return inner

        lax.fori_loop(0, 8 // XU, step, 0)
        done = hs[...].reshape(64, 2, 2, 8, 128)
        rows = pl.ds(pl.multiple_of(pair * 16, 16), 16)
        for half in range(2):
            out_ref[:, half, rows] = done[:, :, half].reshape(64, 16, 128).astype(BF16)

        @pl.when(pair == 0)
        def _():
            fetch.wait()
            store.start()

        return carry

    lax.fori_loop(0, 2, pair_step, 0)
    store.wait()


def same_tile_mask(labels, repeat):
    tokens = TILE * len(labels)
    tile = lax.broadcasted_iota(jnp.int32, (1, tokens), 1) // TILE
    queries = jnp.zeros((1, tokens), jnp.int32)
    for t, label in enumerate(labels):
        queries = jnp.where(tile == t, label, queries)
    queries = jnp.concatenate([queries] * repeat, axis=1)
    rows = [
        jnp.broadcast_to(jnp.where(queries == label, 0.0, -BIG), (TILE, tokens * repeat))
        for label in labels
    ]
    return jnp.concatenate(rows, axis=0)


def y_kernel(occ_ref, in_ref, *refs):
    weight_refs, (keep_ref, send_ref, hs) = refs[:5], refs[5:]
    pen, slab = lax.axis_index("pen"), lax.axis_index("slab")
    core = pen % 2
    first = pl.program_id(0) * ZTS
    hs[...] = in_ref[...].astype(F32).reshape(ZTS * 1024, 128)
    weights = Weights(1, *weight_refs)
    masks = [
        same_tile_mask([label_of(occ_ref, slab, t, first + k) for t in range(8)], 2)
        for k in range(ZTS)
    ]
    places = [pl.ds(k * 1024 + z, 128, stride=8) for k in range(ZTS) for z in range(8)]
    lines = [hs[at, :] for at in places]
    new = staggered(
        [attend_quad(lines[4 * u : 4 * u + 4], weights, masks[u // 2]) for u in range(2 * ZTS)]
    )
    for at, line in zip(places, new):
        hs[at, :] = line
    for k in range(ZTS):
        for p in range(32):
            base = k * 1024 + p * 32
            keep = pl.ds(pl.multiple_of(base + core * 16, 16), 16)
            send = pl.ds(pl.multiple_of(base + 16 - core * 16, 16), 16)
            keep_ref[k, p] = hs[keep, :].astype(BF16)
            send_ref[k, p] = hs[send, :].astype(BF16)


def z_kernel(occ_ref, kept_ref, got_ref, *refs):
    weight_refs, (out_ref,) = refs[:5], refs[5:]
    pen, slab = lax.axis_index("pen"), lax.axis_index("slab")
    first = pen % 2 == 0
    weights = Weights(2, *weight_refs)

    def step(i, carry):
        masks = [
            same_tile_mask([label_of(occ_ref, slab, i * YTS + k, t) for t in range(4)], 4)
            for k in range(YTS)
        ]
        base = i * (4 * YTS)
        lines = []
        for u in range(4 * YTS):
            pair = ([], [])
            for t in range(4):
                for ref in (kept_ref, got_ref):
                    both = ref[t, base + u].astype(F32)
                    pair[0].append(both[:8])
                    pair[1].append(both[8:])
            lines += [jnp.concatenate(pair[0], axis=0), jnp.concatenate(pair[1], axis=0)]
        new = staggered(
            [attend_quad(lines[4 * u : 4 * u + 4], weights, masks[u // 2]) for u in range(2 * YTS)]
        )
        for j in range(8 * YTS):
            for t in range(4):
                kept, got = new[j][t * 16 : t * 16 + 8], new[j][t * 16 + 8 : t * 16 + 16]
                ordered = jnp.concatenate(
                    [jnp.where(first, kept, got), jnp.where(first, got, kept)], axis=0
                )
                rows = slice((j % 2) * 16, (j % 2 + 1) * 16)
                out_ref[t * 32 + base + j // 2, rows, :] = ordered.astype(BF16)
        return carry

    lax.fori_loop(0, 8 // YTS, step, 0)


def merge_kernel(occ_ref, new_ref, res_in_ref, res_ref, sems):
    del res_in_ref
    pen, slab = lax.axis_index("pen"), lax.axis_index("slab")
    tile_y = pen // 4
    copies = []
    for g in range(4):
        start = (g * GROUP + label_of(occ_ref, g, tile_y, slab)) * TILE
        for k in range(4):
            copies.append(
                pltpu.make_async_copy(
                    new_ref.at[pl.ds(g * TILE + k * 4, 4)],
                    res_ref.at[pl.ds(start + k * 4, 4)],
                    sems.at[g * 4 + k],
                )
            )
            copies[-1].start()
    for copy in copies:
        copy.wait()


SMEM = pl.BlockSpec(memory_space=pltpu.SMEM)
VMEM = pl.BlockSpec(memory_space=pltpu.VMEM)
ANY = pl.BlockSpec(memory_space=pl.ANY)
HBM = pl.BlockSpec(memory_space=pltpu.HBM)
PARAMS = pltpu.CompilerParams(vmem_limit_bytes=VMEM_BYTES)


def body(volume, occupancy, gains, w_query, w_key, w_value, w_out):
    params = (gains, w_query, w_key, w_value, w_out)
    occupancy = jnp.transpose(occupancy, (1, 2, 0))
    after_x, copied = pl.pallas_call(
        x_kernel,
        out_shape=(
            jax.ShapeDtypeStruct((64, 2, 32, 128), BF16),
            jax.ShapeDtypeStruct(volume.shape, BF16),
        ),
        in_specs=[SMEM, HBM, *[HBM] * 5],
        out_specs=(VMEM, HBM),
        scratch_shapes=[
            pltpu.VMEM((2, 64, 2, 16, 128), BF16),
            pltpu.VMEM(volume.shape, BF16),
            pltpu.VMEM((64 * 32, 128), F32),
            pltpu.SemaphoreType.DMA((2, 4)),
            pltpu.SemaphoreType.DMA((2,)),
            *[pltpu.VMEM(array.shape, array.dtype) for array in params],
            pltpu.SemaphoreType.DMA((5,)),
        ],
        compiler_params=pltpu.CompilerParams(vmem_limit_bytes=60 * 2**20),
        name="x_phase",
    )(occupancy, volume, *params)

    both = ("slab", "pen")
    planes = lax.all_to_all(after_x.reshape(128, 32, 128), both, 0, 0, tiled=True)

    half = jax.ShapeDtypeStruct((4, 32, 16, 128), BF16)
    half_spec = pl.BlockSpec((ZTS, 32, 16, 128), lambda i: (i, 0, 0, 0))
    kept, sent = pl.pallas_call(
        y_kernel,
        grid=(4 // ZTS,),
        out_shape=(half, half),
        in_specs=[SMEM, pl.BlockSpec((32 * ZTS, 32, 128), lambda i: (i, 0, 0)), *[VMEM] * 5],
        out_specs=(half_spec, half_spec),
        scratch_shapes=[pltpu.VMEM((ZTS * 1024, 128), F32)],
        compiler_params=PARAMS,
        name="y_phase",
    )(occupancy, planes, *params)

    got = lax.ppermute(sent, "pen", [(p, p ^ 1) for p in range(lax.axis_size("pen"))])

    after_z = pl.pallas_call(
        z_kernel,
        out_shape=jax.ShapeDtypeStruct((128, 32, 128), BF16),
        in_specs=[SMEM, VMEM, VMEM, *[VMEM] * 5],
        out_specs=VMEM,
        compiler_params=PARAMS,
        name="z_phase",
    )(occupancy, kept, got, *params)

    home = lax.all_to_all(after_z, both, 0, 0, tiled=True).reshape(64, 4, 16, 128)

    return pl.pallas_call(
        merge_kernel,
        out_shape=jax.ShapeDtypeStruct(volume.shape, BF16),
        in_specs=[SMEM, ANY, HBM],
        out_specs=HBM,
        scratch_shapes=[pltpu.SemaphoreType.DMA((16,))],
        input_output_aliases={2: 0},
        compiler_params=PARAMS,
        name="merge",
    )(occupancy, home, copied)


def solution(mesh):
    placed = (P(None, "pen", "slab", None), P(), P(), P(), P(), P(), P())
    return jax.shard_map(
        body, mesh=mesh, in_specs=placed, out_specs=P(None, "pen", "slab", None), check_vma=False
    )
```

time: 800 us -> 92.4 us (0.12); the launches traced: 791 us -> 92.1 us
  matrix products: 313 us -> 0 us
  other arithmetic: 134 us -> 0 us
  local copies, waits for them, and re-layouts: 121 us -> 0.02 us
  waiting for transfers between devices: 91 us -> 1.54 us
  blocking collectives: 113 us -> 53.4 us
  Pallas kernels: 0 us -> 35.9 us
  starting transfers between devices: 15.5 us -> 1.24 us
    dot_general x128 -> x0, matrix products: 193 us -> none  [the longest x24 129 us: block_attend(): jnp.einsum('bhlm,bmhe->blhe', weights, value_rows, preferred_element_type...]
    sub x16 -> x0, matrix products: 121 us -> none  [block_attend(): exponent = jnp.exp(scores - row_top)]
    all_to_all x2 -> x0, waiting for transfers between devices: 91 us -> none  [the longest x1 47.4 us: body(): lax.all_to_all(section_x, 'pen', split_axis=0, concat_axis=1, tiled=True)]
    all_to_all x2, blocking collectives: 113 us -> 53.4 us  [the longest x1 30.6 us: body(): lax.all_to_all(after_x.reshape(128, 32, 128), both, 0, 0, tiled=True)]
    reduce_sum x48 -> x0, other arithmetic: 55.8 us -> none  [the longest x24 32 us: block_attend(): row_var = jnp.mean(centred * centred, axis=-1, keepdims=True)]
    sub x8 -> x0, other arithmetic: 43.9 us -> none  [block_attend(): exponent = jnp.exp(scores - row_top)]
    pallas_call x0 -> x4, Pallas kernels: none -> 35.9 us  [the longest x1 14.1 us: body(): pl.pallas_call(x_kernel, out_shape=(jax.ShapeDtypeStruct((64, 2, 32, 128)...]
    convert_element_type x24 -> x0, other arithmetic: 32.1 us -> none  [block_attend(): normed = (centred * lax.rsqrt(row_var + 1e-05) * gain).astype(jnp.bfloat16)]
  transfers between devices with their start and end apart: 2 -> 1, of which waited for: 2 -> 1; matrix products, arithmetic and copies ran while one was open for 1% -> 0% of each run, Pallas kernels for 0% -> 0%
where the time goes in v1:
time: 92.4 us; the launch traced here: 92.1 us
  blocking collectives  53.4 us (58%)
  Pallas kernels  35.9 us (39%)
  waiting for transfers between devices  1.54 us (2%)
  starting transfers between devices  1.24 us (1%)
    all_to_all x1, blocking collectives, body(): lax.all_to_all(after_x.reshape(128, 32, 128), both, 0, 0, tiled=True)  30.6 us
    all_to_all x1, blocking collectives, body(): lax.all_to_all(after_z, both, 0, 0, tiled=True).reshape(64, 4, 16, 128)  22.8 us
    pallas_call x1, Pallas kernels, body(): pl.pallas_call(x_kernel, out_shape=(jax.ShapeDtypeStruct((64, 2, 32, 128)...  14.1 us
    pallas_call x1, Pallas kernels, body(): pl.pallas_call(y_kernel, grid=(4 // ZTS,), out_shape=(half, half), in_spe...  10.4 us
    pallas_call x1, Pallas kernels, body(): pl.pallas_call(z_kernel, out_shape=jax.ShapeDtypeStruct((128, 32, 128), B...  9.47 us
    pallas_call x1, Pallas kernels, body(): pl.pallas_call(merge_kernel, out_shape=jax.ShapeDtypeStruct(volume.shape,...  1.91 us
  transfers between devices with their start and end apart: 1, of which 1 were waited for; matrix products, arithmetic and copies ran while one was open for 0% of the time, Pallas kernels for 0%

profile of v1, /device:TPU:1, one launch (start us, length us, event | category | flops | bytes accessed | tf_op | source)
XLA Modules:
  0.0 92.1 jit_solution(13989411506963125223)
XLA Ops:
  0.0 0.0 copy-start.3
  0.0 0.0 copy-start.2
  0.0 0.0 copy-start.1
  0.0 0.0 copy-start
  0.0 0.0 copy-start.5
  0.0 0.0 copy-start.4
  0.0 14.1 %x_phase.1 = (bf16[64,2,32,128]{3,2,1,0:T(8,128)(2,1)}, bf16[256,4,16,128]{3,2,1,0:T(8,128)(2,1)}) custom-call(s32[8,4,16]{2,1,0:T(4,128)} %bitcast.4, bf16[256,4,16,128]{3,2,1,0:T(8,128)(2,1)} %vol_ref.1, f32[3,128]{1,0:T(4,128)} %refs_0_.5, bf16[3,128,128]{2,1,0:T(8,128)(2,1)} %refs_1_.5, bf16[3,128,128]{2,1,0:T(8,128)(2,1)} %refs_2_.5, ...), custom_call_target="tpu_custom_call" | custom-call | tf_op jit(solution)/shard_map/x_phase/pallas_call | solution.py:361
  14.1 30.6 %all_to_all.10.in_ref = bf16[128,32,128]{2,1,0:T(8,128)(2,1)S(1)} all-to-all(bf16[128,32,128]{2,1,0:T(8,128)(2,1)} %bitcast.8), channel_id=1, replica_groups=mesh['slab'=4,'pen'=32] {'slab','pen'}, dimensions={0} | all-to-all | bytes 2097152 | tf_op jit(solution)/shard_map/all_to_all | solution.py:383
  44.7 0.0 copy-done.3
  44.7 0.0 copy-done.2
  44.7 0.0 copy-done.1
  44.7 0.0 copy-done
  44.7 0.0 copy-done.5
  44.7 0.0 copy-done.4
  44.7 10.4 %y_phase.1 = (bf16[4,32,16,128]{3,2,1,0:T(8,128)(2,1)S(1)}, bf16[4,32,16,128]{3,2,1,0:T(8,128)(2,1)S(1)}) custom-call(s32[8,4,16]{2,1,0:T(4,128)S(1)} %bitcast.5, bf16[128,32,128]{2,1,0:T(8,128)(2,1)S(1)} %all_to_all.10.in_ref, f32[3,128]{1,0:T(4,128)S(1)} %copy-done.5, bf16[3,128,128]{2,1,0:T(8,128)(2,1)S(1)} %copy-done, ...), custom_call_target="tpu_custom_call" | custom-call | tf_op jit(solution)/shard_map/y_phase/pallas_call | solution.py:387
  55.2 1.2 %collective-permute-start = (bf16[4,32,16,128]{3,2,1,0:T(8,128)(2,1)S(1)}, bf16[4,32,16,128]{3,2,1,0:T(8,128)(2,1)S(1)}, u32[]{:S(2)}, u32[]{:S(2)}) collective-permute-start(bf16[4,32,16,128]{3,2,1,0:T(8,128)(2,1)S(1)} %get-tuple-element.11), channel_id=1, source_target_pairs={{0,1},{1,0},{2,3},{3,2},{4,5},{5,4},{6,7},{7,6},{8,9},{9,8},{10,11... | collective-permute-start | bytes 1572872 | tf_op jit(solution)/shard_map/ppermute | solution.py:398
  56.4 1.5 %collective-permute-done.got_ref = bf16[4,32,16,128]{3,2,1,0:T(8,128)(2,1)S(1)} collective-permute-done((bf16[4,32,16,128]{3,2,1,0:T(8,128)(2,1)S(1)}, bf16[4,32,16,128]{3,2,1,0:T(8,128)(2,1)S(1)}, u32[]{:S(2)}, u32[]{:S(2)}) %collective-permute-start) | collective-permute-done | bytes 524320 | tf_op jit(solution)/shard_map/ppermute | solution.py:398
  58.0 9.5 %z_phase.1 = bf16[128,32,128]{2,1,0:T(8,128)(2,1)S(1)} custom-call(s32[8,4,16]{2,1,0:T(4,128)S(1)} %bitcast.6, bf16[4,32,16,128]{3,2,1,0:T(8,128)(2,1)S(1)} %get-tuple-element.10.kept_ref, bf16[4,32,16,128]{3,2,1,0:T(8,128)(2,1)S(1)} %collective-permute-done.got_ref, f32[3,128]{1,0:T(4,128)S(1)} %copy-done.5, bf16[3,128,128]{2,1,0:T(8,128)(2,1)S(1)} %copy-done, ...), custom_call_target="tpu_custom_call" | custom-call | tf_op jit(solution)/shard_map/z_phase/pallas_call | solution.py:400
  67.4 22.8 %all_to_all.11 = bf16[128,32,128]{2,1,0:T(8,128)(2,1)S(1)} all-to-all(bf16[128,32,128]{2,1,0:T(8,128)(2,1)S(1)} %z_phase.1), channel_id=1, replica_groups=mesh['slab'=4,'pen'=32] {'slab','pen'}, dimensions={0} | all-to-all | bytes 2097152 | tf_op jit(solution)/shard_map/all_to_all | solution.py:409
  90.2 1.9 %merge.1 = bf16[256,4,16,128]{3,2,1,0:T(8,128)(2,1)} custom-call(s32[8,4,16]{2,1,0:T(4,128)S(1)} %bitcast.7, bf16[64,4,16,128]{3,2,1,0:T(8,128)(2,1)S(1)} %bitcast.3, bf16[256,4,16,128]{3,2,1,0:T(8,128)(2,1)} %get-tuple-element.12.res_in_ref), custom_call_target="tpu_custom_call", output_to_operand_aliasing={{}: (2, {})} | custom-call | tf_op jit(solution)/shard_map/merge/pallas_call | solution.py:411
Async XLA Ops:
  0.0 44.7 %copy-start.3 = (bf16[3,128,128]{2,1,0:T(8,128)(2,1)S(1)}, bf16[3,128,128]{2,1,0:T(8,128)(2,1)}, u32[]{:S(2)}) copy-start(bf16[3,128,128]{2,1,0:T(8,128)(2,1)} %refs_4_.5) | copy-start | bytes 294916
  0.0 44.7 %copy-start.2 = (bf16[3,128,128]{2,1,0:T(8,128)(2,1)S(1)}, bf16[3,128,128]{2,1,0:T(8,128)(2,1)}, u32[]{:S(2)}) copy-start(bf16[3,128,128]{2,1,0:T(8,128)(2,1)} %refs_3_.5) | copy-start | bytes 294916
  0.0 44.7 %copy-start.1 = (bf16[3,128,128]{2,1,0:T(8,128)(2,1)S(1)}, bf16[3,128,128]{2,1,0:T(8,128)(2,1)}, u32[]{:S(2)}) copy-start(bf16[3,128,128]{2,1,0:T(8,128)(2,1)} %refs_2_.5) | copy-start | bytes 294916
  0.0 44.7 %copy-start = (bf16[3,128,128]{2,1,0:T(8,128)(2,1)S(1)}, bf16[3,128,128]{2,1,0:T(8,128)(2,1)}, u32[]{:S(2)}) copy-start(bf16[3,128,128]{2,1,0:T(8,128)(2,1)} %refs_1_.5) | copy-start | bytes 294916
  0.0 44.7 %copy-start.5 = (f32[3,128]{1,0:T(4,128)S(1)}, f32[3,128]{1,0:T(4,128)}, u32[]{:S(2)}) copy-start(f32[3,128]{1,0:T(4,128)} %refs_0_.5) | copy-start | bytes 4612
  0.0 44.7 %copy-start.4 = (s32[16,8,4]{0,2,1:T(4,128)S(1)}, s32[16,8,4]{0,2,1:T(4,128)}, u32[]{:S(2)}) copy-start(s32[16,8,4]{0,2,1:T(4,128)} %param.8) | copy-start | bytes 6148
  55.2 2.8 %collective-permute-start = (bf16[4,32,16,128]{3,2,1,0:T(8,128)(2,1)S(1)}, bf16[4,32,16,128]{3,2,1,0:T(8,128)(2,1)S(1)}, u32[]{:S(2)}, u32[]{:S(2)}) collective-permute-start(bf16[4,32,16,128]{3,2,1,0:T(8,128)(2,1)S(1)} %get-tuple-element.11), channel_id=1, source_target_pairs={{0,1},{1,0},{2,3},{3,2},{4,5},{5,4},{6,7},{7,6},{8,9},{9,8},{10,11... | collective-permute-start | bytes 1572872 | tf_op jit(solution)/shard_map/ppermute | solution.py:398

commit v2 on v1

--- a/solution.py
+++ b/solution.py
@@ -14,9 +14,10 @@
 BF16 = jnp.bfloat16
 F32 = jnp.float32
 BIG = 1e30
-XU = 4
-ZTS = 2
-YTS = 2
+Y_STRIDE = 9
+STRIDE = 36
+XU = 8
+YTS = 4
 GAP = 1
 YIELD_AT = (1,3)
 VMEM_BYTES = 48 * 2**20
@@ -80,7 +81,7 @@
         if started < len(quads) and turn % GAP == 0:
             active.append(started)
             started += 1
-        for which in list(active):
+        for which in list(active)[::-1]:
             try:
                 next(quads[which])
             except StopIteration as stop:
@@ -172,6 +173,7 @@
             if j in YIELD_AT:
                 yield
         gather(*step, probs)
+        yield
         scores = ahead
     yield
     if length == 64:
@@ -195,59 +197,65 @@
 
 
 def x_kernel(occ_ref, vol_ref, *refs):
-    given, (out_ref, res_ref, vin, whole, hs, sems, whole_sems) = refs[:5], refs[5:12]
-    weight_refs, weight_sems = refs[12:17], refs[17]
-    pen, slab = lax.axis_index("pen"), lax.axis_index("slab")
-    tile_y = pen // 4
-    loads = []
+    given, (out_ref, res_ref, vin, whole, hs, done, sems, whole_sems, out_sems) = refs[:5], refs[5:14]
+    weight_refs, weight_sems = refs[14:19], refs[19]
+    chip, slab = lax.axis_index("chip"), lax.axis_index("slab")
+    tile_y = chip // 2
+    tiles = []
     for pair in range(2):
         for g in range(4):
             start = (g * GROUP + label_of(occ_ref, g, tile_y, slab)) * TILE
-            loads.append(
+            tiles.append(
                 pltpu.make_async_copy(
                     vol_ref.at[pl.ds(start, TILE), pl.ds(pair * 2, 2)],
                     vin.at[pair, pl.ds(g * TILE, TILE)],
                     sems.at[pair, g],
                 )
             )
-            loads[-1].start()
-        if pair == 0:
-            for k in range(5):
-                loads.append(pltpu.make_async_copy(given[k], weight_refs[k], weight_sems.at[k]))
-                loads[-1].start()
     fetch = pltpu.make_async_copy(vol_ref, whole, whole_sems.at[0])
     store = pltpu.make_async_copy(whole, res_ref, whole_sems.at[1])
-    fetch.start()
-    for copy in loads:
+    weight_loads = [
+        pltpu.make_async_copy(given[k], weight_refs[k], weight_sems.at[k]) for k in range(5)
+    ]
+    for copy in tiles[:4] + weight_loads + tiles[4:]:
+        copy.start()
+    for copy in weight_loads:
         copy.wait()
     weights = Weights(0, *weight_refs)
-
-    def pair_step(pair, carry):
-        hs[...] = vin[pair].astype(F32).reshape(64 * 32, 128)
+    for copy in tiles[:4]:
+        copy.wait()
+    outs = []
+    for pair in range(2):
+        if pair:
+            for copy in tiles[4:]:
+                copy.wait()
+            fetch.wait()
+            store.start()
+        held = hs.reshape(64, STRIDE, 128)
+        held[:, :32, :] = vin[pair].astype(F32).reshape(64, 32, 128)
+        if pair == 0:
+            fetch.start()
 
         def step(i, inner):
             at = i * (4 * XU)
-            lines = [hs[pl.ds(at + j, 64, stride=32), :] for j in range(4 * XU)]
+            lines = [hs[pl.ds(at + j, 64, stride=STRIDE), :] for j in range(4 * XU)]
             new = staggered([attend_quad(lines[4 * u : 4 * u + 4], weights) for u in range(XU)])
             for j in range(4 * XU):
-                hs[pl.ds(at + j, 64, stride=32), :] = new[j]
+                hs[pl.ds(at + j, 64, stride=STRIDE), :] = new[j]
             return inner
 
         lax.fori_loop(0, 8 // XU, step, 0)
-        done = hs[...].reshape(64, 2, 2, 8, 128)
-        rows = pl.ds(pl.multiple_of(pair * 16, 16), 16)
+        split = held[:, :32, :].reshape(64, 2, 2, 8, 128)
         for half in range(2):
-            out_ref[:, half, rows] = done[:, :, half].reshape(64, 16, 128).astype(BF16)
-
-        @pl.when(pair == 0)
-        def _():
-            fetch.wait()
-            store.start()
-
-        return carry
-
-    lax.fori_loop(0, 2, pair_step, 0)
-    store.wait()
+            done[pair, half] = split[:, :, half].reshape(64, 16, 128).astype(BF16)
+        outs.append(
+            pltpu.make_async_copy(
+                done.at[pair], out_ref.at[:, :, pl.ds(pair * 16, 16)], out_sems.at[pair]
+            )
+        )
+        outs[-1].start()
+    for copy in [store, *outs]:
+        copy.wait()
 
 
 def same_tile_mask(labels, repeat):
@@ -266,35 +274,36 @@
 
 def y_kernel(occ_ref, in_ref, *refs):
     weight_refs, (keep_ref, send_ref, hs) = refs[:5], refs[5:]
-    pen, slab = lax.axis_index("pen"), lax.axis_index("slab")
-    core = pen % 2
-    first = pl.program_id(0) * ZTS
-    hs[...] = in_ref[...].astype(F32).reshape(ZTS * 1024, 128)
+    chip, slab = lax.axis_index("chip"), lax.axis_index("slab")
+    core = lax.axis_index("core")
+    held = hs.reshape(4, 16, 2, 4, Y_STRIDE, 128)
+    for side in range(2):
+        held[:, :, side, :, :8, :] = in_ref[side].astype(F32).reshape(4, 16, 4, 8, 128)
     weights = Weights(1, *weight_refs)
     masks = [
-        same_tile_mask([label_of(occ_ref, slab, t, first + k) for t in range(8)], 2)
-        for k in range(ZTS)
+        same_tile_mask([label_of(occ_ref, slab, t, tile_z) for t in range(8)], 2)
+        for tile_z in range(4)
     ]
-    places = [pl.ds(k * 1024 + z, 128, stride=8) for k in range(ZTS) for z in range(8)]
+    places = [
+        pl.ds(k * 128 * Y_STRIDE + z, 128, stride=Y_STRIDE) for k in range(4) for z in range(8)
+    ]
     lines = [hs[at, :] for at in places]
     new = staggered(
-        [attend_quad(lines[4 * u : 4 * u + 4], weights, masks[u // 2]) for u in range(2 * ZTS)]
+        [attend_quad(lines[4 * u : 4 * u + 4], weights, masks[u // 2]) for u in range(8)]
     )
     for at, line in zip(places, new):
         hs[at, :] = line
-    for k in range(ZTS):
+    for k in range(4):
         for p in range(32):
-            base = k * 1024 + p * 32
-            keep = pl.ds(pl.multiple_of(base + core * 16, 16), 16)
-            send = pl.ds(pl.multiple_of(base + 16 - core * 16, 16), 16)
-            keep_ref[k, p] = hs[keep, :].astype(BF16)
-            send_ref[k, p] = hs[send, :].astype(BF16)
+            for ref, side in ((keep_ref, core), (send_ref, 1 - core)):
+                rows = [held[k, p // 2, p % 2, side * 2 + j, :8, :] for j in range(2)]
+                ref[k, p] = jnp.concatenate(rows, axis=0).astype(BF16)
 
 
 def z_kernel(occ_ref, kept_ref, got_ref, *refs):
     weight_refs, (out_ref,) = refs[:5], refs[5:]
-    pen, slab = lax.axis_index("pen"), lax.axis_index("slab")
-    first = pen % 2 == 0
+    chip, slab = lax.axis_index("chip"), lax.axis_index("slab")
+    first = lax.axis_index("core") == 0
     weights = Weights(2, *weight_refs)
 
     def step(i, carry):
@@ -322,7 +331,8 @@
                     [jnp.where(first, kept, got), jnp.where(first, got, kept)], axis=0
                 )
                 rows = slice((j % 2) * 16, (j % 2 + 1) * 16)
-                out_ref[t * 32 + base + j // 2, rows, :] = ordered.astype(BF16)
+                u = j // 2
+                out_ref[u % 2, t * 16 + base // 2 + u // 2, rows, :] = ordered.astype(BF16)
         return carry
 
     lax.fori_loop(0, 8 // YTS, step, 0)
@@ -330,17 +340,17 @@
 
 def merge_kernel(occ_ref, new_ref, res_in_ref, res_ref, sems):
     del res_in_ref
-    pen, slab = lax.axis_index("pen"), lax.axis_index("slab")
-    tile_y = pen // 4
+    chip, slab = lax.axis_index("chip"), lax.axis_index("slab")
+    tile_y = chip // 2
     copies = []
     for g in range(4):
         start = (g * GROUP + label_of(occ_ref, g, tile_y, slab)) * TILE
-        for k in range(4):
+        for side in range(2):
             copies.append(
                 pltpu.make_async_copy(
-                    new_ref.at[pl.ds(g * TILE + k * 4, 4)],
-                    res_ref.at[pl.ds(start + k * 4, 4)],
-                    sems.at[g * 4 + k],
+                    new_ref.at[side, pl.ds(g * TILE, TILE)],
+                    res_ref.at[pl.ds(start, TILE), pl.ds(side * 2, 2)],
+                    sems.at[g * 2 + side],
                 )
             )
             copies[-1].start()
@@ -361,16 +371,18 @@
     after_x, copied = pl.pallas_call(
         x_kernel,
         out_shape=(
-            jax.ShapeDtypeStruct((64, 2, 32, 128), BF16),
+            jax.ShapeDtypeStruct((2, 64, 32, 128), BF16),
             jax.ShapeDtypeStruct(volume.shape, BF16),
         ),
         in_specs=[SMEM, HBM, *[HBM] * 5],
-        out_specs=(VMEM, HBM),
+        out_specs=(HBM, HBM),
         scratch_shapes=[
             pltpu.VMEM((2, 64, 2, 16, 128), BF16),
             pltpu.VMEM(volume.shape, BF16),
-            pltpu.VMEM((64 * 32, 128), F32),
+            pltpu.VMEM((64 * STRIDE, 128), F32),
+            pltpu.VMEM((2, 2, 64, 16, 128), BF16),
             pltpu.SemaphoreType.DMA((2, 4)),
+            pltpu.SemaphoreType.DMA((2,)),
             pltpu.SemaphoreType.DMA((2,)),
             *[pltpu.VMEM(array.shape, array.dtype) for array in params],
             pltpu.SemaphoreType.DMA((5,)),
@@ -379,49 +391,48 @@
         name="x_phase",
     )(occupancy, volume, *params)
 
-    both = ("slab", "pen")
-    planes = lax.all_to_all(after_x.reshape(128, 32, 128), both, 0, 0, tiled=True)
+    every = ("core", "slab", "chip")
+    planes = lax.all_to_all(after_x.reshape(128, 32, 128), every, 0, 0, tiled=True)
 
     half = jax.ShapeDtypeStruct((4, 32, 16, 128), BF16)
-    half_spec = pl.BlockSpec((ZTS, 32, 16, 128), lambda i: (i, 0, 0, 0))
     kept, sent = pl.pallas_call(
         y_kernel,
-        grid=(4 // ZTS,),
         out_shape=(half, half),
-        in_specs=[SMEM, pl.BlockSpec((32 * ZTS, 32, 128), lambda i: (i, 0, 0)), *[VMEM] * 5],
-        out_specs=(half_spec, half_spec),
-        scratch_shapes=[pltpu.VMEM((ZTS * 1024, 128), F32)],
+        in_specs=[SMEM, VMEM, *[VMEM] * 5],
+        out_specs=(VMEM, VMEM),
+        scratch_shapes=[pltpu.VMEM((4 * 128 * Y_STRIDE, 128), F32)],
         compiler_params=PARAMS,
         name="y_phase",
-    )(occupancy, planes, *params)
-
-    got = lax.ppermute(sent, "pen", [(p, p ^ 1) for p in range(lax.axis_size("pen"))])
+    )(occupancy, planes.reshape(2, 64, 32, 128), *params)
+
+    got = lax.ppermute(sent, "core", [(0, 1), (1, 0)])
 
     after_z = pl.pallas_call(
         z_kernel,
-        out_shape=jax.ShapeDtypeStruct((128, 32, 128), BF16),
+        out_shape=jax.ShapeDtypeStruct((2, 64, 32, 128), BF16),
         in_specs=[SMEM, VMEM, VMEM, *[VMEM] * 5],
         out_specs=VMEM,
         compiler_params=PARAMS,
         name="z_phase",
     )(occupancy, kept, got, *params)
 
-    home = lax.all_to_all(after_z, both, 0, 0, tiled=True).reshape(64, 4, 16, 128)
+    home = lax.all_to_all(after_z.reshape(128, 32, 128), every, 0, 0, tiled=True)
 
     return pl.pallas_call(
         merge_kernel,
         out_shape=jax.ShapeDtypeStruct(volume.shape, BF16),
         in_specs=[SMEM, ANY, HBM],
         out_specs=HBM,
-        scratch_shapes=[pltpu.SemaphoreType.DMA((16,))],
+        scratch_shapes=[pltpu.SemaphoreType.DMA((8,))],
         input_output_aliases={2: 0},
         compiler_params=PARAMS,
         name="merge",
-    )(occupancy, home, copied)
+    )(occupancy, home.reshape(2, 64, 2, 16, 128), copied)
 
 
 def solution(mesh):
-    placed = (P(None, "pen", "slab", None), P(), P(), P(), P(), P(), P())
-    return jax.shard_map(
-        body, mesh=mesh, in_specs=placed, out_specs=P(None, "pen", "slab", None), check_vma=False
-    )
+    devices = mesh.devices.reshape(mesh.shape["slab"], -1, 2)
+    cores = jax.sharding.Mesh(devices, ("slab", "chip", "core"))
+    volume = P(None, ("chip", "core"), "slab", None)
+    placed = (volume, P(), P(), P(), P(), P(), P())
+    return jax.shard_map(body, mesh=cores, in_specs=placed, out_specs=volume, check_vma=False)

time: 92.4 us -> 83.5 us (0.904)
  Pallas kernels: 35.9 us -> 28.3 us
  blocking collectives: 53.4 us -> 51.8 us
    pallas_call x3, Pallas kernels: 34 us -> 26.4 us  [the longest x1 9.95 us: body(): pl.pallas_call(x_kernel, out_shape=(jax.ShapeDtypeStruct((2, 64, 32, 128)...]
    all_to_all x2, blocking collectives: 53.4 us -> 51.8 us  [the longest x1 29.5 us: body(): lax.all_to_all(after_x.reshape(128, 32, 128), every, 0, 0, tiled=True)]
where the time goes in v2:
time: 83.5 us; the launch traced here: 83.2 us
  blocking collectives  51.8 us (62%)
  Pallas kernels  28.3 us (34%)
  waiting for transfers between devices  1.54 us (2%)
  starting transfers between devices  1.28 us (2%)
    all_to_all x1, blocking collectives, body(): lax.all_to_all(after_x.reshape(128, 32, 128), every, 0, 0, tiled=True)  29.5 us
    all_to_all x1, blocking collectives, body(): lax.all_to_all(after_z.reshape(128, 32, 128), every, 0, 0, tiled=True)  22.4 us
    pallas_call x1, Pallas kernels, body(): pl.pallas_call(x_kernel, out_shape=(jax.ShapeDtypeStruct((2, 64, 32, 128)...  9.95 us
    pallas_call x1, Pallas kernels, body(): pl.pallas_call(y_kernel, out_shape=(half, half), in_specs=[SMEM, VMEM, *[...  8.89 us
    pallas_call x1, Pallas kernels, body(): pl.pallas_call(z_kernel, out_shape=jax.ShapeDtypeStruct((2, 64, 32, 128),...  7.57 us
    pallas_call x1, Pallas kernels, body(): pl.pallas_call(merge_kernel, out_shape=jax.ShapeDtypeStruct(volume.shape,...  1.85 us
  transfers between devices with their start and end apart: 1, of which 1 were waited for; matrix products, arithmetic and copies ran while one was open for 0% of the time, Pallas kernels for 0%

profile of v2, /device:TPU:1, one launch (start us, length us, event | category | flops | bytes accessed | tf_op | source)
XLA Modules:
  0.0 83.2 jit_solution(2104406986662866598)
XLA Ops:
  0.0 0.0 copy-start.3
  0.0 0.0 copy-start.2
  0.0 0.0 copy-start.1
  0.0 0.0 copy-start
  0.0 0.0 copy-start.5
  0.0 0.0 copy-start.4
  0.0 9.9 %x_phase.1 = (bf16[2,64,32,128]{3,2,1,0:T(8,128)(2,1)}, bf16[256,4,16,128]{3,2,1,0:T(8,128)(2,1)}) custom-call(s32[8,4,16]{2,1,0:T(4,128)} %bitcast.8, bf16[256,4,16,128]{3,2,1,0:T(8,128)(2,1)} %vol_ref.1, f32[3,128]{1,0:T(4,128)} %refs_0_.5, bf16[3,128,128]{2,1,0:T(8,128)(2,1)} %refs_1_.5, bf16[3,128,128]{2,1,0:T(8,128)(2,1)} %refs_2_.5, ...), custom_call_target="tpu_custom_call" | custom-call | tf_op jit(solution)/shard_map/x_phase/pallas_call | solution.py:371
  10.0 29.5 %all_to_all.10 = bf16[128,32,128]{2,1,0:T(8,128)(2,1)S(1)} all-to-all(bf16[128,32,128]{2,1,0:T(8,128)(2,1)} %bitcast.12), channel_id=1, replica_groups=mesh['slab'=4,'chip'=16,'core'=2] {'core','slab','chip'}, dimensions={0} | all-to-all | bytes 2097152 | tf_op jit(solution)/shard_map/all_to_all | solution.py:395
  39.5 0.0 copy-done.3
  39.5 0.0 copy-done.2
  39.5 0.0 copy-done.1
  39.5 0.0 copy-done
  39.5 0.0 copy-done.5
  39.5 0.0 copy-done.4
  39.5 8.9 %y_phase.1 = (bf16[4,32,16,128]{3,2,1,0:T(8,128)(2,1)S(1)}, bf16[4,32,16,128]{3,2,1,0:T(8,128)(2,1)S(1)}) custom-call(s32[8,4,16]{2,1,0:T(4,128)S(1)} %bitcast.9, bf16[2,64,32,128]{3,2,1,0:T(8,128)(2,1)S(1)} %bitcast.6, f32[3,128]{1,0:T(4,128)S(1)} %copy-done.5, bf16[3,128,128]{2,1,0:T(8,128)(2,1)S(1)} %copy-done, bf16[3,128,128]{2,1,0:T(8,128)(2,1)S(1)} %copy-done.1, ...), custom_call_target="tpu_custom_call" | custom-call | tf_op jit(solution)/shard_map/y_phase/pallas_call | solution.py:398
  48.4 1.3 %collective-permute-start = (bf16[4,32,16,128]{3,2,1,0:T(8,128)(2,1)S(1)}, bf16[4,32,16,128]{3,2,1,0:T(8,128)(2,1)S(1)}, u32[]{:S(2)}, u32[]{:S(2)}) collective-permute-start(bf16[4,32,16,128]{3,2,1,0:T(8,128)(2,1)S(1)} %get-tuple-element.11), channel_id=1, source_target_pairs={{0,1},{1,0},{2,3},{3,2},{4,5},{5,4},{6,7},{7,6},{8,9},{9,8},{10,11... | collective-permute-start | bytes 1572872 | tf_op jit(solution)/shard_map/ppermute | solution.py:408
  49.7 1.5 %collective-permute-done.got_ref = bf16[4,32,16,128]{3,2,1,0:T(8,128)(2,1)S(1)} collective-permute-done((bf16[4,32,16,128]{3,2,1,0:T(8,128)(2,1)S(1)}, bf16[4,32,16,128]{3,2,1,0:T(8,128)(2,1)S(1)}, u32[]{:S(2)}, u32[]{:S(2)}) %collective-permute-start) | collective-permute-done | bytes 524320 | tf_op jit(solution)/shard_map/ppermute | solution.py:408
  51.2 7.6 %z_phase.1 = bf16[2,64,32,128]{3,2,1,0:T(8,128)(2,1)S(1)} custom-call(s32[8,4,16]{2,1,0:T(4,128)S(1)} %bitcast.10, bf16[4,32,16,128]{3,2,1,0:T(8,128)(2,1)S(1)} %get-tuple-element.10.kept_ref, bf16[4,32,16,128]{3,2,1,0:T(8,128)(2,1)S(1)} %collective-permute-done.got_ref, f32[3,128]{1,0:T(4,128)S(1)} %copy-done.5, bf16[3,128,128]{2,1,0:T(8,128)(2,1)S(1)} %copy-done, ...), custom_call_target="tpu_custom_call" | custom-call | tf_op jit(solution)/shard_map/z_phase/pallas_call | solution.py:410
  58.8 22.4 %all_to_all.11 = bf16[128,32,128]{2,1,0:T(8,128)(2,1)S(1)} all-to-all(bf16[128,32,128]{2,1,0:T(8,128)(2,1)S(1)} %bitcast.7), channel_id=1, replica_groups=mesh['slab'=4,'chip'=16,'core'=2] {'core','slab','chip'}, dimensions={0} | all-to-all | bytes 2097152 | tf_op jit(solution)/shard_map/all_to_all | solution.py:419
  81.2 1.9 %merge.1 = bf16[256,4,16,128]{3,2,1,0:T(8,128)(2,1)} custom-call(s32[8,4,16]{2,1,0:T(4,128)S(1)} %bitcast.11, bf16[2,64,2,16,128]{4,3,2,1,0:T(8,128)(2,1)S(1)} %bitcast.5, bf16[256,4,16,128]{3,2,1,0:T(8,128)(2,1)} %get-tuple-element.12.res_in_ref), custom_call_target="tpu_custom_call", output_to_operand_aliasing={{}: (2, {})} | custom-call | tf_op jit(solution)/shard_map/merge/pallas_call | solution.py:421
Async XLA Ops:
  0.0 39.5 %copy-start.3 = (bf16[3,128,128]{2,1,0:T(8,128)(2,1)S(1)}, bf16[3,128,128]{2,1,0:T(8,128)(2,1)}, u32[]{:S(2)}) copy-start(bf16[3,128,128]{2,1,0:T(8,128)(2,1)} %refs_4_.5) | copy-start | bytes 294916
  0.0 39.5 %copy-start.2 = (bf16[3,128,128]{2,1,0:T(8,128)(2,1)S(1)}, bf16[3,128,128]{2,1,0:T(8,128)(2,1)}, u32[]{:S(2)}) copy-start(bf16[3,128,128]{2,1,0:T(8,128)(2,1)} %refs_3_.5) | copy-start | bytes 294916
  0.0 39.5 %copy-start.1 = (bf16[3,128,128]{2,1,0:T(8,128)(2,1)S(1)}, bf16[3,128,128]{2,1,0:T(8,128)(2,1)}, u32[]{:S(2)}) copy-start(bf16[3,128,128]{2,1,0:T(8,128)(2,1)} %refs_2_.5) | copy-start | bytes 294916
  0.0 39.5 %copy-start = (bf16[3,128,128]{2,1,0:T(8,128)(2,1)S(1)}, bf16[3,128,128]{2,1,0:T(8,128)(2,1)}, u32[]{:S(2)}) copy-start(bf16[3,128,128]{2,1,0:T(8,128)(2,1)} %refs_1_.5) | copy-start | bytes 294916
  0.0 39.5 %copy-start.5 = (f32[3,128]{1,0:T(4,128)S(1)}, f32[3,128]{1,0:T(4,128)}, u32[]{:S(2)}) copy-start(f32[3,128]{1,0:T(4,128)} %refs_0_.5) | copy-start | bytes 4612
  0.0 39.5 %copy-start.4 = (s32[16,8,4]{0,2,1:T(4,128)S(1)}, s32[16,8,4]{0,2,1:T(4,128)}, u32[]{:S(2)}) copy-start(s32[16,8,4]{0,2,1:T(4,128)} %param.8) | copy-start | bytes 6148
  48.4 2.8 %collective-permute-start = (bf16[4,32,16,128]{3,2,1,0:T(8,128)(2,1)S(1)}, bf16[4,32,16,128]{3,2,1,0:T(8,128)(2,1)S(1)}, u32[]{:S(2)}, u32[]{:S(2)}) collective-permute-start(bf16[4,32,16,128]{3,2,1,0:T(8,128)(2,1)S(1)} %get-tuple-element.11), channel_id=1, source_target_pairs={{0,1},{1,0},{2,3},{3,2},{4,5},{5,4},{6,7},{7,6},{8,9},{9,8},{10,11... | collective-permute-start | bytes 1572872 | tf_op jit(solution)/shard_map/ppermute | solution.py:408

commit v3 on v2

--- a/solution.py
+++ b/solution.py
@@ -16,18 +16,15 @@
 BIG = 1e30
 Y_STRIDE = 9
 STRIDE = 36
-XU = 8
-YTS = 4
 GAP = 1
-YIELD_AT = (1,3)
 VMEM_BYTES = 48 * 2**20
 
 
 def normalise(rows, gain):
-    mean = jnp.mean(rows, axis=-1, keepdims=True)
-    centred = rows - mean
-    var = jnp.mean(centred * centred, axis=-1, keepdims=True)
-    return (centred * lax.rsqrt(var + 1e-05) * gain).astype(BF16)
+    width = rows.shape[1]
+    centred = rows - jnp.sum(rows, axis=-1, keepdims=True) * (1.0 / width)
+    total = jnp.sum(centred * centred, axis=-1, keepdims=True)
+    return (centred * lax.rsqrt(total + 1e-05 * width) * gain).astype(BF16)
 
 
 def dot_nt(a, b):
@@ -67,7 +64,7 @@
 
 class Weights:
     def __init__(self, phase, gain_ref, w_query_ref, w_key_ref, w_value_ref, w_out_ref):
-        self.gain = gain_ref[phase : phase + 1, :]
+        self.gain = gain_ref[phase : phase + 1, :] * math.sqrt(128)
         self.query = paired(w_query_ref[phase])
         self.key = paired(w_key_ref[phase])
         self.value_t = w_value_ref[phase].astype(F32).T.astype(BF16)
@@ -124,7 +121,7 @@
 
     def weights_of(line):
         if mask is not None:
-            line = line + mask
+            line = line + mask()
         top = jnp.max(line, axis=0, keepdims=True)
         line = jnp.exp2((line - top) * (math.log2(math.e) / math.sqrt(head_size)))
         return (line * (1.0 / jnp.sum(line, axis=0, keepdims=True))).astype(BF16)
@@ -170,7 +167,7 @@
         probs = []
         for j in range(4):
             probs.append(weights_of(scores[j * length : (j + 1) * length]))
-            if j in YIELD_AT:
+            if length == 128:
                 yield
         gather(*step, probs)
         yield
@@ -196,94 +193,93 @@
     return label
 
 
+def tile_labels(occ_ref, group):
+    index = lax.broadcasted_iota(jnp.int32, (1, 1, occ_ref.shape[2]), 2)
+    place = jnp.where(index // GROUP == group, index % GROUP, 0)
+    return jnp.sum((occ_ref[...] * place).astype(F32), axis=-1, keepdims=True)
+
+
+def same_tile_mask(labels, rows):
+    made = []
+
+    def mask():
+        if not made:
+            keys = jnp.concatenate([jnp.broadcast_to(label, (TILE, 128)) for label in labels], axis=0)
+            one = jnp.where(keys == keys.T, 0.0, -BIG)[:rows]
+            made.append(jnp.concatenate([one, one], axis=1))
+        return made[0]
+
+    return mask
+
+
 def x_kernel(occ_ref, vol_ref, *refs):
-    given, (out_ref, res_ref, vin, whole, hs, done, sems, whole_sems, out_sems) = refs[:5], refs[5:14]
-    weight_refs, weight_sems = refs[14:19], refs[19]
+    given, (out_ref, res_ref, starts_out) = refs[:5], refs[5:8]
+    vin, whole, hs, done, starts, occ, sems, whole_sems, out_sems, table_sems = refs[8:18]
+    weight_refs, weight_sems = refs[18:23], refs[23]
     chip, slab = lax.axis_index("chip"), lax.axis_index("slab")
     tile_y = chip // 2
+    occ_load = pltpu.make_async_copy(occ_ref, occ, table_sems.at[1])
+    occ_load.start()
+    weight_loads = [
+        pltpu.make_async_copy(given[0], weight_refs[0], weight_sems.at[0]),
+        *[
+            pltpu.make_async_copy(given[k].at[pl.ds(0, 1)], weight_refs[k], weight_sems.at[k])
+            for k in range(1, 5)
+        ],
+    ]
+    for copy in weight_loads:
+        copy.start()
+    occ_load.wait()
     tiles = []
-    for pair in range(2):
-        for g in range(4):
-            start = (g * GROUP + label_of(occ_ref, g, tile_y, slab)) * TILE
-            tiles.append(
-                pltpu.make_async_copy(
-                    vol_ref.at[pl.ds(start, TILE), pl.ds(pair * 2, 2)],
-                    vin.at[pair, pl.ds(g * TILE, TILE)],
-                    sems.at[pair, g],
-                )
+    for g in range(4):
+        start = (g * GROUP + label_of(occ, g, tile_y, slab)) * TILE
+        starts[g : g + 1, :] = jnp.full((1, 128), start, jnp.int32)
+        tiles.append(
+            pltpu.make_async_copy(
+                vol_ref.at[pl.ds(start, TILE)], vin.at[pl.ds(g * TILE, TILE)], sems.at[g]
             )
+        )
     fetch = pltpu.make_async_copy(vol_ref, whole, whole_sems.at[0])
     store = pltpu.make_async_copy(whole, res_ref, whole_sems.at[1])
-    weight_loads = [
-        pltpu.make_async_copy(given[k], weight_refs[k], weight_sems.at[k]) for k in range(5)
-    ]
-    for copy in tiles[:4] + weight_loads + tiles[4:]:
+    for copy in tiles:
         copy.start()
+    starts_copy = pltpu.make_async_copy(starts, starts_out, table_sems.at[0])
+    starts_copy.start()
     for copy in weight_loads:
         copy.wait()
     weights = Weights(0, *weight_refs)
-    for copy in tiles[:4]:
+    for copy in tiles:
         copy.wait()
+    fetch.start()
     outs = []
-    for pair in range(2):
-        if pair:
-            for copy in tiles[4:]:
-                copy.wait()
+    held = hs.reshape(64, STRIDE, 128)
+    places = [pl.ds(j, 64, stride=STRIDE) for j in range(32)]
+    for half in range(2):
+        rows = vin[:, :, half * 8 : (half + 1) * 8, :].astype(F32)
+        held[:, :32, :] = rows.reshape(64, 32, 128)
+        lines = [hs[at, :] for at in places]
+        new = staggered([attend_quad(lines[4 * u : 4 * u + 4], weights) for u in range(8)])
+        for at, line in zip(places, new):
+            hs[at, :] = line
+        done[half] = held[:, :32, :].astype(BF16)
+        outs.append(pltpu.make_async_copy(done.at[half], out_ref.at[half], out_sems.at[half]))
+        outs[-1].start()
+        if half == 0:
             fetch.wait()
             store.start()
-        held = hs.reshape(64, STRIDE, 128)
-        held[:, :32, :] = vin[pair].astype(F32).reshape(64, 32, 128)
-        if pair == 0:
-            fetch.start()
-
-        def step(i, inner):
-            at = i * (4 * XU)
-            lines = [hs[pl.ds(at + j, 64, stride=STRIDE), :] for j in range(4 * XU)]
-            new = staggered([attend_quad(lines[4 * u : 4 * u + 4], weights) for u in range(XU)])
-            for j in range(4 * XU):
-                hs[pl.ds(at + j, 64, stride=STRIDE), :] = new[j]
-            return inner
-
-        lax.fori_loop(0, 8 // XU, step, 0)
-        split = held[:, :32, :].reshape(64, 2, 2, 8, 128)
-        for half in range(2):
-            done[pair, half] = split[:, :, half].reshape(64, 16, 128).astype(BF16)
-        outs.append(
-            pltpu.make_async_copy(
-                done.at[pair], out_ref.at[:, :, pl.ds(pair * 16, 16)], out_sems.at[pair]
-            )
-        )
-        outs[-1].start()
-    for copy in [store, *outs]:
+    for copy in [store, *outs, starts_copy]:
         copy.wait()
-
-
-def same_tile_mask(labels, repeat):
-    tokens = TILE * len(labels)
-    tile = lax.broadcasted_iota(jnp.int32, (1, tokens), 1) // TILE
-    queries = jnp.zeros((1, tokens), jnp.int32)
-    for t, label in enumerate(labels):
-        queries = jnp.where(tile == t, label, queries)
-    queries = jnp.concatenate([queries] * repeat, axis=1)
-    rows = [
-        jnp.broadcast_to(jnp.where(queries == label, 0.0, -BIG), (TILE, tokens * repeat))
-        for label in labels
-    ]
-    return jnp.concatenate(rows, axis=0)
 
 
 def y_kernel(occ_ref, in_ref, *refs):
     weight_refs, (keep_ref, send_ref, hs) = refs[:5], refs[5:]
-    chip, slab = lax.axis_index("chip"), lax.axis_index("slab")
     core = lax.axis_index("core")
     held = hs.reshape(4, 16, 2, 4, Y_STRIDE, 128)
     for side in range(2):
         held[:, :, side, :, :8, :] = in_ref[side].astype(F32).reshape(4, 16, 4, 8, 128)
     weights = Weights(1, *weight_refs)
-    masks = [
-        same_tile_mask([label_of(occ_ref, slab, t, tile_z) for t in range(8)], 2)
-        for tile_z in range(4)
-    ]
+    labels = tile_labels(occ_ref, lax.axis_index("slab"))
+    masks = [same_tile_mask([labels[k, t : t + 1] for k in range(8)], 128) for t in range(4)]
     places = [
         pl.ds(k * 128 * Y_STRIDE + z, 128, stride=Y_STRIDE) for k in range(4) for z in range(8)
     ]
@@ -302,49 +298,42 @@
 
 def z_kernel(occ_ref, kept_ref, got_ref, *refs):
     weight_refs, (out_ref,) = refs[:5], refs[5:]
-    chip, slab = lax.axis_index("chip"), lax.axis_index("slab")
     first = lax.axis_index("core") == 0
     weights = Weights(2, *weight_refs)
 
-    def step(i, carry):
-        masks = [
-            same_tile_mask([label_of(occ_ref, slab, i * YTS + k, t) for t in range(4)], 4)
-            for k in range(YTS)
-        ]
-        base = i * (4 * YTS)
-        lines = []
-        for u in range(4 * YTS):
-            pair = ([], [])
-            for t in range(4):
-                for ref in (kept_ref, got_ref):
-                    both = ref[t, base + u].astype(F32)
-                    pair[0].append(both[:8])
-                    pair[1].append(both[8:])
-            lines += [jnp.concatenate(pair[0], axis=0), jnp.concatenate(pair[1], axis=0)]
-        new = staggered(
-            [attend_quad(lines[4 * u : 4 * u + 4], weights, masks[u // 2]) for u in range(2 * YTS)]
-        )
-        for j in range(8 * YTS):
-            for t in range(4):
-                kept, got = new[j][t * 16 : t * 16 + 8], new[j][t * 16 + 8 : t * 16 + 16]
-                ordered = jnp.concatenate(
-                    [jnp.where(first, kept, got), jnp.where(first, got, kept)], axis=0
-                )
-                rows = slice((j % 2) * 16, (j % 2 + 1) * 16)
-                u = j // 2
-                out_ref[u % 2, t * 16 + base // 2 + u // 2, rows, :] = ordered.astype(BF16)
-        return carry
-
-    lax.fori_loop(0, 8 // YTS, step, 0)
-
-
-def merge_kernel(occ_ref, new_ref, res_in_ref, res_ref, sems):
+    labels = tile_labels(occ_ref, lax.axis_index("slab"))
+    masks = [
+        same_tile_mask([labels[k, t : t + 1] for t in range(4)] * 2, 64) for k in range(8)
+    ]
+    lines = []
+    for u in range(32):
+        pair = ([], [])
+        for t in range(4):
+            for ref in (kept_ref, got_ref):
+                both = ref[t, u].astype(F32)
+                pair[0].append(both[:8])
+                pair[1].append(both[8:])
+        lines += [jnp.concatenate(pair[0], axis=0), jnp.concatenate(pair[1], axis=0)]
+    new = staggered(
+        [attend_quad(lines[4 * u : 4 * u + 4], weights, masks[u // 2]) for u in range(16)]
+    )
+    for j in range(64):
+        for t in range(4):
+            kept, got = new[j][t * 16 : t * 16 + 8], new[j][t * 16 + 8 : t * 16 + 16]
+            ordered = jnp.concatenate(
+                [jnp.where(first, kept, got), jnp.where(first, got, kept)], axis=0
+            )
+            rows = slice((j % 2) * 16, (j % 2 + 1) * 16)
+            u = j // 2
+            out_ref[u % 2, t * 16 + u // 2, rows, :] = ordered.astype(BF16)
+
+
+def merge_kernel(starts_ref, new_ref, res_in_ref, res_ref, sems):
     del res_in_ref
-    chip, slab = lax.axis_index("chip"), lax.axis_index("slab")
-    tile_y = chip // 2
+    starts = starts_ref[...]
     copies = []
     for g in range(4):
-        start = (g * GROUP + label_of(occ_ref, g, tile_y, slab)) * TILE
+        start = pl.multiple_of(starts[g, 0], TILE)
         for side in range(2):
             copies.append(
                 pltpu.make_async_copy(
@@ -358,7 +347,6 @@
         copy.wait()
 
 
-SMEM = pl.BlockSpec(memory_space=pltpu.SMEM)
 VMEM = pl.BlockSpec(memory_space=pltpu.VMEM)
 ANY = pl.BlockSpec(memory_space=pl.ANY)
 HBM = pl.BlockSpec(memory_space=pltpu.HBM)
@@ -368,23 +356,29 @@
 def body(volume, occupancy, gains, w_query, w_key, w_value, w_out):
     params = (gains, w_query, w_key, w_value, w_out)
     occupancy = jnp.transpose(occupancy, (1, 2, 0))
-    after_x, copied = pl.pallas_call(
+    table = jax.ShapeDtypeStruct((8, 128), jnp.int32)
+    after_x, copied, starts = pl.pallas_call(
         x_kernel,
         out_shape=(
             jax.ShapeDtypeStruct((2, 64, 32, 128), BF16),
             jax.ShapeDtypeStruct(volume.shape, BF16),
+            table,
         ),
-        in_specs=[SMEM, HBM, *[HBM] * 5],
-        out_specs=(HBM, HBM),
+        in_specs=[HBM, HBM, *[HBM] * 5],
+        out_specs=(HBM,) * 3,
         scratch_shapes=[
-            pltpu.VMEM((2, 64, 2, 16, 128), BF16),
+            pltpu.VMEM((64, 4, 16, 128), BF16),
             pltpu.VMEM(volume.shape, BF16),
             pltpu.VMEM((64 * STRIDE, 128), F32),
-            pltpu.VMEM((2, 2, 64, 16, 128), BF16),
-            pltpu.SemaphoreType.DMA((2, 4)),
+            pltpu.VMEM((2, 64, 32, 128), BF16),
+            pltpu.VMEM(table.shape, table.dtype),
+            pltpu.SMEM(occupancy.shape, jnp.int32),
+            pltpu.SemaphoreType.DMA((4,)),
             pltpu.SemaphoreType.DMA((2,)),
             pltpu.SemaphoreType.DMA((2,)),
-            *[pltpu.VMEM(array.shape, array.dtype) for array in params],
+            pltpu.SemaphoreType.DMA((2,)),
+            pltpu.VMEM(gains.shape, gains.dtype),
+            *[pltpu.VMEM((1, *array.shape[1:]), array.dtype) for array in params[1:]],
             pltpu.SemaphoreType.DMA((5,)),
         ],
         compiler_params=pltpu.CompilerParams(vmem_limit_bytes=60 * 2**20),
@@ -398,7 +392,7 @@
     kept, sent = pl.pallas_call(
         y_kernel,
         out_shape=(half, half),
-        in_specs=[SMEM, VMEM, *[VMEM] * 5],
+        in_specs=[VMEM] * 7,
         out_specs=(VMEM, VMEM),
         scratch_shapes=[pltpu.VMEM((4 * 128 * Y_STRIDE, 128), F32)],
         compiler_params=PARAMS,
@@ -410,7 +404,7 @@
     after_z = pl.pallas_call(
         z_kernel,
         out_shape=jax.ShapeDtypeStruct((2, 64, 32, 128), BF16),
-        in_specs=[SMEM, VMEM, VMEM, *[VMEM] * 5],
+        in_specs=[VMEM] * 8,
         out_specs=VMEM,
         compiler_params=PARAMS,
         name="z_phase",
@@ -421,13 +415,13 @@
     return pl.pallas_call(
         merge_kernel,
         out_shape=jax.ShapeDtypeStruct(volume.shape, BF16),
-        in_specs=[SMEM, ANY, HBM],
+        in_specs=[VMEM, ANY, HBM],
         out_specs=HBM,
         scratch_shapes=[pltpu.SemaphoreType.DMA((8,))],
         input_output_aliases={2: 0},
         compiler_params=PARAMS,
         name="merge",
-    )(occupancy, home.reshape(2, 64, 2, 16, 128), copied)
+    )(starts, home.reshape(2, 64, 2, 16, 128), copied)
 
 
 def solution(mesh):

time: 83.5 us -> 80.5 us (0.964)
  Pallas kernels: 28.3 us -> 25.1 us
    pallas_call x1, Pallas kernels: 7.57 us -> 5.85 us  [body(): pl.pallas_call(z_kernel, out_shape=jax.ShapeDtypeStruct((2, 64, 32, 128),...]
where the time goes in v3:
time: 80.5 us; the launch traced here: 80.2 us
  blocking collectives  51.8 us (64%)
  Pallas kernels  25.1 us (31%)
  waiting for transfers between devices  1.54 us (2%)
  starting transfers between devices  1.51 us (2%)
    all_to_all x1, blocking collectives, body(): lax.all_to_all(after_x.reshape(128, 32, 128), every, 0, 0, tiled=True)  29.4 us
    all_to_all x1, blocking collectives, body(): lax.all_to_all(after_z.reshape(128, 32, 128), every, 0, 0, tiled=True)  22.4 us
    pallas_call x1, Pallas kernels, body(): pl.pallas_call(x_kernel, out_shape=(jax.ShapeDtypeStruct((2, 64, 32, 128)...  9.48 us
    pallas_call x1, Pallas kernels, body(): pl.pallas_call(y_kernel, out_shape=(half, half), in_specs=[VMEM] * 7, out...  8.67 us
    pallas_call x1, Pallas kernels, body(): pl.pallas_call(z_kernel, out_shape=jax.ShapeDtypeStruct((2, 64, 32, 128),...  5.85 us
  transfers between devices with their start and end apart: 1, of which 1 were waited for; matrix products, arithmetic and copies ran while one was open for 0% of the time, Pallas kernels for 0%

profile of v3, /device:TPU:1, one launch (start us, length us, event | category | flops | bytes accessed | tf_op | source)
XLA Modules:
  0.0 80.2 jit_solution(178204006048069552)
XLA Ops:
  0.0 0.0 copy-start.3
  0.0 0.0 copy-start.2
  0.0 0.0 copy-start.1
  0.0 0.0 copy-start
  0.0 0.0 copy-start.5
  0.0 0.0 copy-start.4
  0.0 9.5 %x_phase.1 = (bf16[2,64,32,128]{3,2,1,0:T(8,128)(2,1)}, bf16[256,4,16,128]{3,2,1,0:T(8,128)(2,1)}, s32[8,128]{1,0:T(8,128)}) custom-call(s32[8,4,16]{2,1,0:T(4,128)} %bitcast.8, bf16[256,4,16,128]{3,2,1,0:T(8,128)(2,1)} %vol_ref.1, f32[3,128]{1,0:T(4,128)} %refs_0_.5, bf16[3,128,128]{2,1,0:T(8,128)(2,1)} %refs_1_.5, bf16[3,128,128]{2,1,0:T(8,128)(2,1)} %refs_2_.5, ...), custom_call_target="tpu_custom_call" | custom-call | tf_op jit(solution)/shard_map/x_phase/pallas_call | solution.py:360
  9.5 0.0 copy-start.6
  9.5 29.4 %all_to_all.10 = bf16[128,32,128]{2,1,0:T(8,128)(2,1)S(1)} all-to-all(bf16[128,32,128]{2,1,0:T(8,128)(2,1)} %bitcast.11), channel_id=1, replica_groups=mesh['slab'=4,'chip'=16,'core'=2] {'core','slab','chip'}, dimensions={0} | all-to-all | bytes 2097152 | tf_op jit(solution)/shard_map/all_to_all | solution.py:389
  39.0 0.0 copy-done.3
  39.0 0.0 copy-done.2
  39.0 0.0 copy-done.1
  39.0 0.0 copy-done
  39.0 0.0 copy-done.5
  39.0 0.0 copy-done.4
  39.0 8.7 %y_phase.1 = (bf16[4,32,16,128]{3,2,1,0:T(8,128)(2,1)S(1)}, bf16[4,32,16,128]{3,2,1,0:T(8,128)(2,1)S(1)}) custom-call(s32[8,4,16]{2,1,0:T(4,128)S(1)} %bitcast.9, bf16[2,64,32,128]{3,2,1,0:T(8,128)(2,1)S(1)} %bitcast.6, f32[3,128]{1,0:T(4,128)S(1)} %copy-done.5, bf16[3,128,128]{2,1,0:T(8,128)(2,1)S(1)} %copy-done, bf16[3,128,128]{2,1,0:T(8,128)(2,1)S(1)} %copy-done.1, ...), custom_call_target="tpu_custom_call" | custom-call | tf_op jit(solution)/shard_map/y_phase/pallas_call | solution.py:392
  47.7 1.5 %collective-permute-start = (bf16[4,32,16,128]{3,2,1,0:T(8,128)(2,1)S(1)}, bf16[4,32,16,128]{3,2,1,0:T(8,128)(2,1)S(1)}, u32[]{:S(2)}, u32[]{:S(2)}) collective-permute-start(bf16[4,32,16,128]{3,2,1,0:T(8,128)(2,1)S(1)} %get-tuple-element.13), channel_id=1, source_target_pairs={{0,1},{1,0},{2,3},{3,2},{4,5},{5,4},{6,7},{7,6},{8,9},{9,8},{10,11... | collective-permute-start | bytes 1572872 | tf_op jit(solution)/shard_map/ppermute | solution.py:402
  49.2 1.5 %collective-permute-done.got_ref = bf16[4,32,16,128]{3,2,1,0:T(8,128)(2,1)S(1)} collective-permute-done((bf16[4,32,16,128]{3,2,1,0:T(8,128)(2,1)S(1)}, bf16[4,32,16,128]{3,2,1,0:T(8,128)(2,1)S(1)}, u32[]{:S(2)}, u32[]{:S(2)}) %collective-permute-start) | collective-permute-done | bytes 524320 | tf_op jit(solution)/shard_map/ppermute | solution.py:402
  50.7 5.8 %z_phase.1 = bf16[2,64,32,128]{3,2,1,0:T(8,128)(2,1)S(1)} custom-call(s32[8,4,16]{2,1,0:T(4,128)S(1)} %bitcast.10, bf16[4,32,16,128]{3,2,1,0:T(8,128)(2,1)S(1)} %get-tuple-element.12.kept_ref, bf16[4,32,16,128]{3,2,1,0:T(8,128)(2,1)S(1)} %collective-permute-done.got_ref, f32[3,128]{1,0:T(4,128)S(1)} %copy-done.5, bf16[3,128,128]{2,1,0:T(8,128)(2,1)S(1)} %copy-done, ...), custom_call_target="tpu_custom_call" | custom-call | tf_op jit(solution)/shard_map/z_phase/pallas_call | solution.py:404
  56.6 22.4 %all_to_all.11 = bf16[128,32,128]{2,1,0:T(8,128)(2,1)S(1)} all-to-all(bf16[128,32,128]{2,1,0:T(8,128)(2,1)S(1)} %bitcast.7), channel_id=1, replica_groups=mesh['slab'=4,'chip'=16,'core'=2] {'core','slab','chip'}, dimensions={0} | all-to-all | bytes 2097152 | tf_op jit(solution)/shard_map/all_to_all | solution.py:413
  79.0 0.0 copy-done.6
  79.0 1.1 %merge.1 = bf16[256,4,16,128]{3,2,1,0:T(8,128)(2,1)} custom-call(s32[8,128]{1,0:T(8,128)S(1)} %copy-done.6, bf16[2,64,2,16,128]{4,3,2,1,0:T(8,128)(2,1)S(1)} %bitcast.5, bf16[256,4,16,128]{3,2,1,0:T(8,128)(2,1)} %get-tuple-element.14.res_in_ref), custom_call_target="tpu_custom_call", output_to_operand_aliasing={{}: (2, {})} | custom-call | tf_op jit(solution)/shard_map/merge/pallas_call | solution.py:415
Async XLA Ops:
  0.0 39.0 %copy-start.3 = (bf16[3,128,128]{2,1,0:T(8,128)(2,1)S(1)}, bf16[3,128,128]{2,1,0:T(8,128)(2,1)}, u32[]{:S(2)}) copy-start(bf16[3,128,128]{2,1,0:T(8,128)(2,1)} %refs_4_.5) | copy-start | bytes 294916
  0.0 39.0 %copy-start.2 = (bf16[3,128,128]{2,1,0:T(8,128)(2,1)S(1)}, bf16[3,128,128]{2,1,0:T(8,128)(2,1)}, u32[]{:S(2)}) copy-start(bf16[3,128,128]{2,1,0:T(8,128)(2,1)} %refs_3_.5) | copy-start | bytes 294916
  0.0 39.0 %copy-start.1 = (bf16[3,128,128]{2,1,0:T(8,128)(2,1)S(1)}, bf16[3,128,128]{2,1,0:T(8,128)(2,1)}, u32[]{:S(2)}) copy-start(bf16[3,128,128]{2,1,0:T(8,128)(2,1)} %refs_2_.5) | copy-start | bytes 294916
  0.0 39.0 %copy-start = (bf16[3,128,128]{2,1,0:T(8,128)(2,1)S(1)}, bf16[3,128,128]{2,1,0:T(8,128)(2,1)}, u32[]{:S(2)}) copy-start(bf16[3,128,128]{2,1,0:T(8,128)(2,1)} %refs_1_.5) | copy-start | bytes 294916
  0.0 39.0 %copy-start.5 = (f32[3,128]{1,0:T(4,128)S(1)}, f32[3,128]{1,0:T(4,128)}, u32[]{:S(2)}) copy-start(f32[3,128]{1,0:T(4,128)} %refs_0_.5) | copy-start | bytes 4612
  0.0 39.0 %copy-start.4 = (s32[16,8,4]{0,2,1:T(4,128)S(1)}, s32[16,8,4]{0,2,1:T(4,128)}, u32[]{:S(2)}) copy-start(s32[16,8,4]{0,2,1:T(4,128)} %param.8) | copy-start | bytes 6148
  9.5 69.4 %copy-start.6 = (s32[8,128]{1,0:T(8,128)S(1)}, s32[8,128]{1,0:T(8,128)}, u32[]{:S(2)}) copy-start(s32[8,128]{1,0:T(8,128)} %get-tuple-element.10.starts_ref) | copy-start | bytes 12292
  47.7 3.1 %collective-permute-start = (bf16[4,32,16,128]{3,2,1,0:T(8,128)(2,1)S(1)}, bf16[4,32,16,128]{3,2,1,0:T(8,128)(2,1)S(1)}, u32[]{:S(2)}, u32[]{:S(2)}) collective-permute-start(bf16[4,32,16,128]{3,2,1,0:T(8,128)(2,1)S(1)} %get-tuple-element.13), channel_id=1, source_target_pairs={{0,1},{1,0},{2,3},{3,2},{4,5},{5,4},{6,7},{7,6},{8,9},{9,8},{10,11... | collective-permute-start | bytes 1572872 | tf_op jit(solution)/shard_map/ppermute | solution.py:402

commit v4 on v3

--- a/solution.py
+++ b/solution.py
@@ -71,8 +71,7 @@
         self.out = w_out_ref[phase]
 
 
-def staggered(quads):
-    results = [None] * len(quads)
+def staggered(quads, finish):
     active, turn, started = [], 0, 0
     while active or started < len(quads):
         if started < len(quads) and turn % GAP == 0:
@@ -82,13 +81,13 @@
             try:
                 next(quads[which])
             except StopIteration as stop:
-                results[which] = stop.value
                 active.remove(which)
+                finish(which, stop.value)
         turn += 1
-    return sum(results, [])
-
-
-def attend_quad(lines, weights, mask=None):
+
+
+def attend_quad(load, weights, mask=None):
+    lines = load()
     length, width = lines[0].shape
     head_size = width // HEADS
     per_tile = 256 // length
@@ -173,6 +172,7 @@
         yield
         scores = ahead
     yield
+    lines = load()
     if length == 64:
         new = []
         for pair in range(2):
@@ -193,23 +193,16 @@
     return label
 
 
-def tile_labels(occ_ref, group):
+def tile_marks(occ_ref, group):
     index = lax.broadcasted_iota(jnp.int32, (1, 1, occ_ref.shape[2]), 2)
-    place = jnp.where(index // GROUP == group, index % GROUP, 0)
-    return jnp.sum((occ_ref[...] * place).astype(F32), axis=-1, keepdims=True)
-
-
-def same_tile_mask(labels, rows):
-    made = []
-
-    def mask():
-        if not made:
-            keys = jnp.concatenate([jnp.broadcast_to(label, (TILE, 128)) for label in labels], axis=0)
-            one = jnp.where(keys == keys.T, 0.0, -BIG)[:rows]
-            made.append(jnp.concatenate([one, one], axis=1))
-        return made[0]
-
-    return mask
+    return jnp.where(index // GROUP == group, occ_ref[...], 0).astype(F32)
+
+
+def same_tile_mask(mask_ref, marks):
+    marks = jnp.concatenate([jnp.broadcast_to(m, (TILE, m.shape[1])) for m in marks], axis=0)
+    marks = marks.astype(BF16)
+    mask_ref[...] = (dot_nt(marks[: mask_ref.shape[0]], marks) - 1.0) * BIG
+    return lambda: jnp.concatenate([mask_ref[...]] * 2, axis=1)
 
 
 def x_kernel(occ_ref, vol_ref, *refs):
@@ -252,80 +245,112 @@
         copy.wait()
     fetch.start()
     outs = []
-    held = hs.reshape(64, STRIDE, 128)
-    places = [pl.ds(j, 64, stride=STRIDE) for j in range(32)]
-    for half in range(2):
-        rows = vin[:, :, half * 8 : (half + 1) * 8, :].astype(F32)
-        held[:, :32, :] = rows.reshape(64, 32, 128)
-        lines = [hs[at, :] for at in places]
-        new = staggered([attend_quad(lines[4 * u : 4 * u + 4], weights) for u in range(8)])
-        for at, line in zip(places, new):
-            hs[at, :] = line
-        done[half] = held[:, :32, :].astype(BF16)
-        outs.append(pltpu.make_async_copy(done.at[half], out_ref.at[half], out_sems.at[half]))
-        outs[-1].start()
-        if half == 0:
-            fetch.wait()
-            store.start()
+    held = hs.reshape(2, 64, STRIDE, 128)
+
+    def load_quad(u):
+        half = u // 8
+        asked = []
+
+        def load():
+            if u % 8 == 0 and not asked:
+                rows = vin[:, :, half * 8 : (half + 1) * 8, :].astype(F32)
+                held[half, :, :32, :] = rows.reshape(64, 32, 128)
+            if u == 15 and not asked:
+                fetch.wait()
+                store.start()
+            asked.append(u)
+            return [hs[place(u, j), :] for j in range(4)]
+
+        return load
+
+    def place(u, j):
+        return pl.ds((u // 8) * 64 * STRIDE + (u % 8) * 4 + j, 64, stride=STRIDE)
+
+    def finish(u, new):
+        for j in range(4):
+            hs[place(u, j), :] = new[j]
+        if u % 8 == 7:
+            half = u // 8
+            done[half] = held[half, :, :32, :].astype(BF16)
+            outs.append(pltpu.make_async_copy(done.at[half], out_ref.at[half], out_sems.at[half]))
+            outs[-1].start()
+
+    staggered([attend_quad(load_quad(u), weights) for u in range(16)], finish)
     for copy in [store, *outs, starts_copy]:
         copy.wait()
 
 
 def y_kernel(occ_ref, in_ref, *refs):
-    weight_refs, (keep_ref, send_ref, hs) = refs[:5], refs[5:]
+    weight_refs, (keep_ref, send_ref, hs, mask_ref) = refs[:5], refs[5:]
     core = lax.axis_index("core")
     held = hs.reshape(4, 16, 2, 4, Y_STRIDE, 128)
     for side in range(2):
         held[:, :, side, :, :8, :] = in_ref[side].astype(F32).reshape(4, 16, 4, 8, 128)
     weights = Weights(1, *weight_refs)
-    labels = tile_labels(occ_ref, lax.axis_index("slab"))
-    masks = [same_tile_mask([labels[k, t : t + 1] for k in range(8)], 128) for t in range(4)]
-    places = [
-        pl.ds(k * 128 * Y_STRIDE + z, 128, stride=Y_STRIDE) for k in range(4) for z in range(8)
+    marks = tile_marks(occ_ref, lax.axis_index("slab"))
+    masks = [
+        same_tile_mask(mask_ref.at[t], [marks[k, t : t + 1] for k in range(8)]) for t in range(4)
     ]
-    lines = [hs[at, :] for at in places]
-    new = staggered(
-        [attend_quad(lines[4 * u : 4 * u + 4], weights, masks[u // 2]) for u in range(8)]
-    )
-    for at, line in zip(places, new):
-        hs[at, :] = line
-    for k in range(4):
-        for p in range(32):
-            for ref, side in ((keep_ref, core), (send_ref, 1 - core)):
-                rows = [held[k, p // 2, p % 2, side * 2 + j, :8, :] for j in range(2)]
-                ref[k, p] = jnp.concatenate(rows, axis=0).astype(BF16)
+
+    def place(u, j):
+        return pl.ds((u // 2) * 128 * Y_STRIDE + (u % 2) * 4 + j, 128, stride=Y_STRIDE)
+
+    def load_quad(u):
+        return lambda: [hs[place(u, j), :] for j in range(4)]
+
+    def finish(u, new):
+        for j in range(4):
+            hs[place(u, j), :] = new[j]
+        if u % 2:
+            k = u // 2
+            for p in range(32):
+                for ref, side in ((keep_ref, core), (send_ref, 1 - core)):
+                    rows = [held[k, p // 2, p % 2, side * 2 + j, :8, :] for j in range(2)]
+                    ref[k, p] = jnp.concatenate(rows, axis=0).astype(BF16)
+
+    staggered([attend_quad(load_quad(u), weights, masks[u // 2]) for u in range(8)], finish)
 
 
 def z_kernel(occ_ref, kept_ref, got_ref, *refs):
-    weight_refs, (out_ref,) = refs[:5], refs[5:]
+    weight_refs, (out_ref, mask_ref) = refs[:5], refs[5:]
     first = lax.axis_index("core") == 0
     weights = Weights(2, *weight_refs)
 
-    labels = tile_labels(occ_ref, lax.axis_index("slab"))
+    marks = tile_marks(occ_ref, lax.axis_index("slab"))
     masks = [
-        same_tile_mask([labels[k, t : t + 1] for t in range(4)] * 2, 64) for k in range(8)
+        same_tile_mask(mask_ref.at[k], [marks[k, t : t + 1] for t in range(4)] * 2)
+        for k in range(8)
     ]
-    lines = []
-    for u in range(32):
-        pair = ([], [])
-        for t in range(4):
-            for ref in (kept_ref, got_ref):
-                both = ref[t, u].astype(F32)
-                pair[0].append(both[:8])
-                pair[1].append(both[8:])
-        lines += [jnp.concatenate(pair[0], axis=0), jnp.concatenate(pair[1], axis=0)]
-    new = staggered(
-        [attend_quad(lines[4 * u : 4 * u + 4], weights, masks[u // 2]) for u in range(16)]
-    )
-    for j in range(64):
-        for t in range(4):
-            kept, got = new[j][t * 16 : t * 16 + 8], new[j][t * 16 + 8 : t * 16 + 16]
-            ordered = jnp.concatenate(
-                [jnp.where(first, kept, got), jnp.where(first, got, kept)], axis=0
-            )
-            rows = slice((j % 2) * 16, (j % 2 + 1) * 16)
-            u = j // 2
-            out_ref[u % 2, t * 16 + u // 2, rows, :] = ordered.astype(BF16)
+
+    def load_quad(quad):
+        lines = []
+
+        def load():
+            if not lines:
+                for u in (quad * 2, quad * 2 + 1):
+                    pair = ([], [])
+                    for t in range(4):
+                        for ref in (kept_ref, got_ref):
+                            both = ref[t, u].astype(F32)
+                            pair[0].append(both[:8])
+                            pair[1].append(both[8:])
+                    lines.extend(jnp.concatenate(rows, axis=0) for rows in pair)
+            return lines
+
+        return load
+
+    def finish(quad, new):
+        for j in range(4):
+            u = quad * 2 + j // 2
+            for t in range(4):
+                kept, got = new[j][t * 16 : t * 16 + 8], new[j][t * 16 + 8 : t * 16 + 16]
+                ordered = jnp.concatenate(
+                    [jnp.where(first, kept, got), jnp.where(first, got, kept)], axis=0
+                )
+                rows = slice((j % 2) * 16, (j % 2 + 1) * 16)
+                out_ref[u % 2, t * 16 + u // 2, rows, :] = ordered.astype(BF16)
+
+    staggered([attend_quad(load_quad(u), weights, masks[u // 2]) for u in range(16)], finish)
 
 
 def merge_kernel(starts_ref, new_ref, res_in_ref, res_ref, sems):
@@ -369,7 +394,7 @@
         scratch_shapes=[
             pltpu.VMEM((64, 4, 16, 128), BF16),
             pltpu.VMEM(volume.shape, BF16),
-            pltpu.VMEM((64 * STRIDE, 128), F32),
+            pltpu.VMEM((2 * 64 * STRIDE, 128), F32),
             pltpu.VMEM((2, 64, 32, 128), BF16),
             pltpu.VMEM(table.shape, table.dtype),
             pltpu.SMEM(occupancy.shape, jnp.int32),
@@ -394,7 +419,10 @@
         out_shape=(half, half),
         in_specs=[VMEM] * 7,
         out_specs=(VMEM, VMEM),
-        scratch_shapes=[pltpu.VMEM((4 * 128 * Y_STRIDE, 128), F32)],
+        scratch_shapes=[
+            pltpu.VMEM((4 * 128 * Y_STRIDE, 128), F32),
+            pltpu.VMEM((4, 128, 128), F32),
+        ],
         compiler_params=PARAMS,
         name="y_phase",
     )(occupancy, planes.reshape(2, 64, 32, 128), *params)
@@ -406,6 +434,7 @@
         out_shape=jax.ShapeDtypeStruct((2, 64, 32, 128), BF16),
         in_specs=[VMEM] * 8,
         out_specs=VMEM,
+        scratch_shapes=[pltpu.VMEM((8, 64, 128), F32)],
         compiler_params=PARAMS,
         name="z_phase",
     )(occupancy, kept, got, *params)

time: 80.5 us -> 79.4 us (0.986)
  Pallas kernels: 25.1 us -> 24 us
where the time goes in v4:
time: 79.4 us; the launch traced here: 79.2 us
  blocking collectives  51.8 us (65%)
  Pallas kernels  24 us (30%)
  waiting for transfers between devices  1.54 us (2%)
  starting transfers between devices  1.51 us (2%)
    all_to_all x1, blocking collectives, body(): lax.all_to_all(after_x.reshape(128, 32, 128), every, 0, 0, tiled=True)  29.5 us
    all_to_all x1, blocking collectives, body(): lax.all_to_all(after_z.reshape(128, 32, 128), every, 0, 0, tiled=True)  22.4 us
    pallas_call x1, Pallas kernels, body(): pl.pallas_call(x_kernel, out_shape=(jax.ShapeDtypeStruct((2, 64, 32, 128)...  8.92 us
    pallas_call x1, Pallas kernels, body(): pl.pallas_call(y_kernel, out_shape=(half, half), in_specs=[VMEM] * 7, out...  8.09 us
    pallas_call x1, Pallas kernels, body(): pl.pallas_call(z_kernel, out_shape=jax.ShapeDtypeStruct((2, 64, 32, 128),...  5.91 us
  transfers between devices with their start and end apart: 1, of which 1 were waited for; matrix products, arithmetic and copies ran while one was open for 0% of the time, Pallas kernels for 0%

profile of v4, /device:TPU:1, one launch (start us, length us, event | category | flops | bytes accessed | tf_op | source)
XLA Modules:
  0.0 79.2 jit_solution(9977071508601951521)
XLA Ops:
  0.0 0.0 copy-start.3
  0.0 0.0 copy-start.2
  0.0 0.0 copy-start.1
  0.0 0.0 copy-start
  0.0 0.0 copy-start.5
  0.0 0.0 copy-start.4
  0.0 8.9 %x_phase.1 = (bf16[2,64,32,128]{3,2,1,0:T(8,128)(2,1)}, bf16[256,4,16,128]{3,2,1,0:T(8,128)(2,1)}, s32[8,128]{1,0:T(8,128)}) custom-call(s32[8,4,16]{2,1,0:T(4,128)} %bitcast.8, bf16[256,4,16,128]{3,2,1,0:T(8,128)(2,1)} %vol_ref.1, f32[3,128]{1,0:T(4,128)} %refs_0_.5, bf16[3,128,128]{2,1,0:T(8,128)(2,1)} %refs_1_.5, bf16[3,128,128]{2,1,0:T(8,128)(2,1)} %refs_2_.5, ...), custom_call_target="tpu_custom_call" | custom-call | tf_op jit(solution)/shard_map/x_phase/pallas_call | solution.py:385
  9.0 0.0 copy-start.6
  9.0 29.5 %all_to_all.10 = bf16[128,32,128]{2,1,0:T(8,128)(2,1)S(1)} all-to-all(bf16[128,32,128]{2,1,0:T(8,128)(2,1)} %bitcast.11), channel_id=1, replica_groups=mesh['slab'=4,'chip'=16,'core'=2] {'core','slab','chip'}, dimensions={0} | all-to-all | bytes 2097152 | tf_op jit(solution)/shard_map/all_to_all | solution.py:414
  38.4 0.0 copy-done.3
  38.4 0.0 copy-done.2
  38.4 0.0 copy-done.1
  38.4 0.0 copy-done
  38.5 0.0 copy-done.5
  38.5 0.0 copy-done.4
  38.5 8.1 %y_phase.1 = (bf16[4,32,16,128]{3,2,1,0:T(8,128)(2,1)S(1)}, bf16[4,32,16,128]{3,2,1,0:T(8,128)(2,1)S(1)}) custom-call(s32[8,4,16]{2,1,0:T(4,128)S(1)} %bitcast.9, bf16[2,64,32,128]{3,2,1,0:T(8,128)(2,1)S(1)} %bitcast.6, f32[3,128]{1,0:T(4,128)S(1)} %copy-done.5, bf16[3,128,128]{2,1,0:T(8,128)(2,1)S(1)} %copy-done, bf16[3,128,128]{2,1,0:T(8,128)(2,1)S(1)} %copy-done.1, ...), custom_call_target="tpu_custom_call" | custom-call | tf_op jit(solution)/shard_map/y_phase/pallas_call | solution.py:417
  46.6 1.5 %collective-permute-start = (bf16[4,32,16,128]{3,2,1,0:T(8,128)(2,1)S(1)}, bf16[4,32,16,128]{3,2,1,0:T(8,128)(2,1)S(1)}, u32[]{:S(2)}, u32[]{:S(2)}) collective-permute-start(bf16[4,32,16,128]{3,2,1,0:T(8,128)(2,1)S(1)} %get-tuple-element.13), channel_id=1, source_target_pairs={{0,1},{1,0},{2,3},{3,2},{4,5},{5,4},{6,7},{7,6},{8,9},{9,8},{10,11... | collective-permute-start | bytes 1572872 | tf_op jit(solution)/shard_map/ppermute | solution.py:430
  48.1 1.5 %collective-permute-done.got_ref = bf16[4,32,16,128]{3,2,1,0:T(8,128)(2,1)S(1)} collective-permute-done((bf16[4,32,16,128]{3,2,1,0:T(8,128)(2,1)S(1)}, bf16[4,32,16,128]{3,2,1,0:T(8,128)(2,1)S(1)}, u32[]{:S(2)}, u32[]{:S(2)}) %collective-permute-start) | collective-permute-done | bytes 524320 | tf_op jit(solution)/shard_map/ppermute | solution.py:430
  49.6 5.9 %z_phase.1 = bf16[2,64,32,128]{3,2,1,0:T(8,128)(2,1)S(1)} custom-call(s32[8,4,16]{2,1,0:T(4,128)S(1)} %bitcast.10, bf16[4,32,16,128]{3,2,1,0:T(8,128)(2,1)S(1)} %get-tuple-element.12.kept_ref, bf16[4,32,16,128]{3,2,1,0:T(8,128)(2,1)S(1)} %collective-permute-done.got_ref, f32[3,128]{1,0:T(4,128)S(1)} %copy-done.5, bf16[3,128,128]{2,1,0:T(8,128)(2,1)S(1)} %copy-done, ...), custom_call_target="tpu_custom_call" | custom-call | tf_op jit(solution)/shard_map/z_phase/pallas_call | solution.py:432
  55.5 22.4 %all_to_all.11 = bf16[128,32,128]{2,1,0:T(8,128)(2,1)S(1)} all-to-all(bf16[128,32,128]{2,1,0:T(8,128)(2,1)S(1)} %bitcast.7), channel_id=1, replica_groups=mesh['slab'=4,'chip'=16,'core'=2] {'core','slab','chip'}, dimensions={0} | all-to-all | bytes 2097152 | tf_op jit(solution)/shard_map/all_to_all | solution.py:442
  77.9 0.0 copy-done.6
  77.9 1.1 %merge.1 = bf16[256,4,16,128]{3,2,1,0:T(8,128)(2,1)} custom-call(s32[8,128]{1,0:T(8,128)S(1)} %copy-done.6, bf16[2,64,2,16,128]{4,3,2,1,0:T(8,128)(2,1)S(1)} %bitcast.5, bf16[256,4,16,128]{3,2,1,0:T(8,128)(2,1)} %get-tuple-element.14.res_in_ref), custom_call_target="tpu_custom_call", output_to_operand_aliasing={{}: (2, {})} | custom-call | tf_op jit(solution)/shard_map/merge/pallas_call | solution.py:444
Async XLA Ops:
  0.0 38.4 %copy-start.3 = (bf16[3,128,128]{2,1,0:T(8,128)(2,1)S(1)}, bf16[3,128,128]{2,1,0:T(8,128)(2,1)}, u32[]{:S(2)}) copy-start(bf16[3,128,128]{2,1,0:T(8,128)(2,1)} %refs_4_.5) | copy-start | bytes 294916
  0.0 38.4 %copy-start.2 = (bf16[3,128,128]{2,1,0:T(8,128)(2,1)S(1)}, bf16[3,128,128]{2,1,0:T(8,128)(2,1)}, u32[]{:S(2)}) copy-start(bf16[3,128,128]{2,1,0:T(8,128)(2,1)} %refs_3_.5) | copy-start | bytes 294916
  0.0 38.4 %copy-start.1 = (bf16[3,128,128]{2,1,0:T(8,128)(2,1)S(1)}, bf16[3,128,128]{2,1,0:T(8,128)(2,1)}, u32[]{:S(2)}) copy-start(bf16[3,128,128]{2,1,0:T(8,128)(2,1)} %refs_2_.5) | copy-start | bytes 294916
  0.0 38.4 %copy-start = (bf16[3,128,128]{2,1,0:T(8,128)(2,1)S(1)}, bf16[3,128,128]{2,1,0:T(8,128)(2,1)}, u32[]{:S(2)}) copy-start(bf16[3,128,128]{2,1,0:T(8,128)(2,1)} %refs_1_.5) | copy-start | bytes 294916
  0.0 38.4 %copy-start.5 = (f32[3,128]{1,0:T(4,128)S(1)}, f32[3,128]{1,0:T(4,128)}, u32[]{:S(2)}) copy-start(f32[3,128]{1,0:T(4,128)} %refs_0_.5) | copy-start | bytes 4612
  0.0 38.4 %copy-start.4 = (s32[16,8,4]{0,2,1:T(4,128)S(1)}, s32[16,8,4]{0,2,1:T(4,128)}, u32[]{:S(2)}) copy-start(s32[16,8,4]{0,2,1:T(4,128)} %param.8) | copy-start | bytes 6148
  9.0 69.0 %copy-start.6 = (s32[8,128]{1,0:T(8,128)S(1)}, s32[8,128]{1,0:T(8,128)}, u32[]{:S(2)}) copy-start(s32[8,128]{1,0:T(8,128)} %get-tuple-element.10.starts_ref) | copy-start | bytes 12292
  46.6 3.0 %collective-permute-start = (bf16[4,32,16,128]{3,2,1,0:T(8,128)(2,1)S(1)}, bf16[4,32,16,128]{3,2,1,0:T(8,128)(2,1)S(1)}, u32[]{:S(2)}, u32[]{:S(2)}) collective-permute-start(bf16[4,32,16,128]{3,2,1,0:T(8,128)(2,1)S(1)} %get-tuple-element.13), channel_id=1, source_target_pairs={{0,1},{1,0},{2,3},{3,2},{4,5},{5,4},{6,7},{7,6},{8,9},{9,8},{10,11... | collective-permute-start | bytes 1572872 | tf_op jit(solution)/shard_map/ppermute | solution.py:430

commit v5 on v4

--- a/solution.py
+++ b/solution.py
@@ -84,6 +84,32 @@
                 active.remove(which)
                 finish(which, stop.value)
         turn += 1
+
+
+class SpareLanes:
+    def __init__(self, marks):
+        marks = jnp.concatenate([jnp.broadcast_to(m, (TILE, m.shape[1])) for m in marks], axis=0)
+        marks = marks.astype(BF16)
+        lane = lane_of(128)
+        row = lax.broadcasted_iota(jnp.int32, (marks.shape[1], 1), 0)
+        self.keys, self.queries = [], []
+        for t in range(2):
+            at = (lane % 64) - 32 * (1 - t)
+            wide = dot_nn(marks, ones_where(at == row))
+            inside = jnp.logical_and(at >= 0, at < marks.shape[1])
+            other = (wide - jnp.where(inside, 1.0, 0.0)) * BIG
+            self.queries.append(jnp.concatenate([other, other], axis=1).astype(BF16))
+            self.keys.append([jnp.where(lane // 64 == j, wide, 0.0).astype(BF16) for j in range(2)])
+
+    def spread(self, query, t, lanes):
+        return jnp.where(lanes, query, self.queries[t])
+
+    def place(self, key, t, j):
+        lane = lane_of(128)
+        own = jnp.logical_and(lane // 64 == j % 2, (lane % 64) // 32 == t)
+        tile = jnp.where(own, key[:, (j // 2) * 128 : (j // 2 + 1) * 128], self.keys[t][j % 2])
+        rest = jnp.zeros_like(tile)
+        return jnp.concatenate([tile, rest] if j < 2 else [rest, tile], axis=1)
 
 
 def attend_quad(load, weights, mask=None):
@@ -112,6 +138,11 @@
         lanes = slice(half * 128, (half + 1) * 128)
         query_half = jnp.concatenate([query[:length, lanes], query[length:, lanes]], axis=1)
         key_half = jnp.concatenate([key[:length, lanes], key[length:, lanes]], axis=1)
+        if length == 128:
+            key_rows = jnp.concatenate([mask.place(key_half, t, j) for j in range(4)], axis=0)
+            heads = [(lane % 64) // head_size == t * per_tile + i for i in range(per_tile)]
+            spread = jnp.concatenate([mask.spread(query_half, t, h) for h in heads], axis=0)
+            return dot_nt(key_rows, spread)
         key_rows = jnp.concatenate([placed(key_half, j, halves) for j in range(4)], axis=0)
         spread = jnp.concatenate(
             [query_half * head_masks[t * per_tile + i] for i in range(per_tile)], axis=0
@@ -119,7 +150,7 @@
         return dot_nt(key_rows, spread)
 
     def weights_of(line):
-        if mask is not None:
+        if mask is not None and length == 64:
             line = line + mask()
         top = jnp.max(line, axis=0, keepdims=True)
         line = jnp.exp2((line - top) * (math.log2(math.e) / math.sqrt(head_size)))
@@ -281,16 +312,14 @@
 
 
 def y_kernel(occ_ref, in_ref, *refs):
-    weight_refs, (keep_ref, send_ref, hs, mask_ref) = refs[:5], refs[5:]
+    weight_refs, (keep_ref, send_ref, hs) = refs[:5], refs[5:]
     core = lax.axis_index("core")
     held = hs.reshape(4, 16, 2, 4, Y_STRIDE, 128)
     for side in range(2):
         held[:, :, side, :, :8, :] = in_ref[side].astype(F32).reshape(4, 16, 4, 8, 128)
     weights = Weights(1, *weight_refs)
     marks = tile_marks(occ_ref, lax.axis_index("slab"))
-    masks = [
-        same_tile_mask(mask_ref.at[t], [marks[k, t : t + 1] for k in range(8)]) for t in range(4)
-    ]
+    masks = [SpareLanes([marks[k, t : t + 1] for k in range(8)]) for t in range(4)]
 
     def place(u, j):
         return pl.ds((u // 2) * 128 * Y_STRIDE + (u % 2) * 4 + j, 128, stride=Y_STRIDE)
@@ -419,10 +448,7 @@
         out_shape=(half, half),
         in_specs=[VMEM] * 7,
         out_specs=(VMEM, VMEM),
-        scratch_shapes=[
-            pltpu.VMEM((4 * 128 * Y_STRIDE, 128), F32),
-            pltpu.VMEM((4, 128, 128), F32),
-        ],
+        scratch_shapes=[pltpu.VMEM((4 * 128 * Y_STRIDE, 128), F32)],
         compiler_params=PARAMS,
         name="y_phase",
     )(occupancy, planes.reshape(2, 64, 32, 128), *params)

time: 79.4 us -> 79 us (level)
  no operation moved by 1% of the time
where the time goes in v5:
time: 79 us; the launch traced here: 78.8 us
  blocking collectives  51.8 us (66%)
  Pallas kernels  23.6 us (30%)
  waiting for transfers between devices  1.54 us (2%)
  starting transfers between devices  1.51 us (2%)
    all_to_all x1, blocking collectives, body(): lax.all_to_all(after_x.reshape(128, 32, 128), every, 0, 0, tiled=True)  29.5 us
    all_to_all x1, blocking collectives, body(): lax.all_to_all(after_z.reshape(128, 32, 128), every, 0, 0, tiled=True)  22.4 us
    pallas_call x1, Pallas kernels, body(): pl.pallas_call(x_kernel, out_shape=(jax.ShapeDtypeStruct((2, 64, 32, 128)...  8.92 us
    pallas_call x1, Pallas kernels, body(): pl.pallas_call(y_kernel, out_shape=(half, half), in_specs=[VMEM] * 7, out...  7.71 us
    pallas_call x1, Pallas kernels, body(): pl.pallas_call(z_kernel, out_shape=jax.ShapeDtypeStruct((2, 64, 32, 128),...  5.92 us
  transfers between devices with their start and end apart: 1, of which 1 were waited for; matrix products, arithmetic and copies ran while one was open for 0% of the time, Pallas kernels for 0%

profile of v5, /device:TPU:1, one launch (start us, length us, event | category | flops | bytes accessed | tf_op | source)
XLA Modules:
  0.0 78.8 jit_solution(8785754742274210840)
XLA Ops:
  0.0 0.0 copy-start.3
  0.0 0.0 copy-start.2
  0.0 0.0 copy-start.1
  0.0 0.0 copy-start
  0.0 0.0 copy-start.5
  0.0 0.0 copy-start.4
  0.0 8.9 %x_phase.1 = (bf16[2,64,32,128]{3,2,1,0:T(8,128)(2,1)}, bf16[256,4,16,128]{3,2,1,0:T(8,128)(2,1)}, s32[8,128]{1,0:T(8,128)}) custom-call(s32[8,4,16]{2,1,0:T(4,128)} %bitcast.8, bf16[256,4,16,128]{3,2,1,0:T(8,128)(2,1)} %vol_ref.1, f32[3,128]{1,0:T(4,128)} %refs_0_.5, bf16[3,128,128]{2,1,0:T(8,128)(2,1)} %refs_1_.5, bf16[3,128,128]{2,1,0:T(8,128)(2,1)} %refs_2_.5, ...), custom_call_target="tpu_custom_call" | custom-call | tf_op jit(solution)/shard_map/x_phase/pallas_call | solution.py:414
  9.0 0.0 copy-start.6
  9.0 29.5 %all_to_all.10 = bf16[128,32,128]{2,1,0:T(8,128)(2,1)S(1)} all-to-all(bf16[128,32,128]{2,1,0:T(8,128)(2,1)} %bitcast.11), channel_id=1, replica_groups=mesh['slab'=4,'chip'=16,'core'=2] {'core','slab','chip'}, dimensions={0} | all-to-all | bytes 2097152 | tf_op jit(solution)/shard_map/all_to_all | solution.py:443
  38.4 0.0 copy-done.3
  38.4 0.0 copy-done.2
  38.4 0.0 copy-done.1
  38.4 0.0 copy-done
  38.5 0.0 copy-done.5
  38.5 0.0 copy-done.4
  38.5 7.7 %y_phase.1 = (bf16[4,32,16,128]{3,2,1,0:T(8,128)(2,1)S(1)}, bf16[4,32,16,128]{3,2,1,0:T(8,128)(2,1)S(1)}) custom-call(s32[8,4,16]{2,1,0:T(4,128)S(1)} %bitcast.9, bf16[2,64,32,128]{3,2,1,0:T(8,128)(2,1)S(1)} %bitcast.6, f32[3,128]{1,0:T(4,128)S(1)} %copy-done.5, bf16[3,128,128]{2,1,0:T(8,128)(2,1)S(1)} %copy-done, bf16[3,128,128]{2,1,0:T(8,128)(2,1)S(1)} %copy-done.1, ...), custom_call_target="tpu_custom_call" | custom-call | tf_op jit(solution)/shard_map/y_phase/pallas_call | solution.py:446
  46.2 1.5 %collective-permute-start = (bf16[4,32,16,128]{3,2,1,0:T(8,128)(2,1)S(1)}, bf16[4,32,16,128]{3,2,1,0:T(8,128)(2,1)S(1)}, u32[]{:S(2)}, u32[]{:S(2)}) collective-permute-start(bf16[4,32,16,128]{3,2,1,0:T(8,128)(2,1)S(1)} %get-tuple-element.13), channel_id=1, source_target_pairs={{0,1},{1,0},{2,3},{3,2},{4,5},{5,4},{6,7},{7,6},{8,9},{9,8},{10,11... | collective-permute-start | bytes 1572872 | tf_op jit(solution)/shard_map/ppermute | solution.py:456
  47.7 1.5 %collective-permute-done.got_ref = bf16[4,32,16,128]{3,2,1,0:T(8,128)(2,1)S(1)} collective-permute-done((bf16[4,32,16,128]{3,2,1,0:T(8,128)(2,1)S(1)}, bf16[4,32,16,128]{3,2,1,0:T(8,128)(2,1)S(1)}, u32[]{:S(2)}, u32[]{:S(2)}) %collective-permute-start) | collective-permute-done | bytes 524320 | tf_op jit(solution)/shard_map/ppermute | solution.py:456
  49.2 5.9 %z_phase.1 = bf16[2,64,32,128]{3,2,1,0:T(8,128)(2,1)S(1)} custom-call(s32[8,4,16]{2,1,0:T(4,128)S(1)} %bitcast.10, bf16[4,32,16,128]{3,2,1,0:T(8,128)(2,1)S(1)} %get-tuple-element.12.kept_ref, bf16[4,32,16,128]{3,2,1,0:T(8,128)(2,1)S(1)} %collective-permute-done.got_ref, f32[3,128]{1,0:T(4,128)S(1)} %copy-done.5, bf16[3,128,128]{2,1,0:T(8,128)(2,1)S(1)} %copy-done, ...), custom_call_target="tpu_custom_call" | custom-call | tf_op jit(solution)/shard_map/z_phase/pallas_call | solution.py:458
  55.2 22.4 %all_to_all.11 = bf16[128,32,128]{2,1,0:T(8,128)(2,1)S(1)} all-to-all(bf16[128,32,128]{2,1,0:T(8,128)(2,1)S(1)} %bitcast.7), channel_id=1, replica_groups=mesh['slab'=4,'chip'=16,'core'=2] {'core','slab','chip'}, dimensions={0} | all-to-all | bytes 2097152 | tf_op jit(solution)/shard_map/all_to_all | solution.py:468
  77.5 0.0 copy-done.6
  77.5 1.1 %merge.1 = bf16[256,4,16,128]{3,2,1,0:T(8,128)(2,1)} custom-call(s32[8,128]{1,0:T(8,128)S(1)} %copy-done.6, bf16[2,64,2,16,128]{4,3,2,1,0:T(8,128)(2,1)S(1)} %bitcast.5, bf16[256,4,16,128]{3,2,1,0:T(8,128)(2,1)} %get-tuple-element.14.res_in_ref), custom_call_target="tpu_custom_call", output_to_operand_aliasing={{}: (2, {})} | custom-call | tf_op jit(solution)/shard_map/merge/pallas_call | solution.py:470
Async XLA Ops:
  0.0 38.4 %copy-start.3 = (bf16[3,128,128]{2,1,0:T(8,128)(2,1)S(1)}, bf16[3,128,128]{2,1,0:T(8,128)(2,1)}, u32[]{:S(2)}) copy-start(bf16[3,128,128]{2,1,0:T(8,128)(2,1)} %refs_4_.5) | copy-start | bytes 294916
  0.0 38.4 %copy-start.2 = (bf16[3,128,128]{2,1,0:T(8,128)(2,1)S(1)}, bf16[3,128,128]{2,1,0:T(8,128)(2,1)}, u32[]{:S(2)}) copy-start(bf16[3,128,128]{2,1,0:T(8,128)(2,1)} %refs_3_.5) | copy-start | bytes 294916
  0.0 38.4 %copy-start.1 = (bf16[3,128,128]{2,1,0:T(8,128)(2,1)S(1)}, bf16[3,128,128]{2,1,0:T(8,128)(2,1)}, u32[]{:S(2)}) copy-start(bf16[3,128,128]{2,1,0:T(8,128)(2,1)} %refs_2_.5) | copy-start | bytes 294916
  0.0 38.4 %copy-start = (bf16[3,128,128]{2,1,0:T(8,128)(2,1)S(1)}, bf16[3,128,128]{2,1,0:T(8,128)(2,1)}, u32[]{:S(2)}) copy-start(bf16[3,128,128]{2,1,0:T(8,128)(2,1)} %refs_1_.5) | copy-start | bytes 294916
  0.0 38.4 %copy-start.5 = (f32[3,128]{1,0:T(4,128)S(1)}, f32[3,128]{1,0:T(4,128)}, u32[]{:S(2)}) copy-start(f32[3,128]{1,0:T(4,128)} %refs_0_.5) | copy-start | bytes 4612
  0.0 38.4 %copy-start.4 = (s32[16,8,4]{0,2,1:T(4,128)S(1)}, s32[16,8,4]{0,2,1:T(4,128)}, u32[]{:S(2)}) copy-start(s32[16,8,4]{0,2,1:T(4,128)} %param.8) | copy-start | bytes 6148
  9.0 68.6 %copy-start.6 = (s32[8,128]{1,0:T(8,128)S(1)}, s32[8,128]{1,0:T(8,128)}, u32[]{:S(2)}) copy-start(s32[8,128]{1,0:T(8,128)} %get-tuple-element.10.starts_ref) | copy-start | bytes 12292
  46.2 3.0 %collective-permute-start = (bf16[4,32,16,128]{3,2,1,0:T(8,128)(2,1)S(1)}, bf16[4,32,16,128]{3,2,1,0:T(8,128)(2,1)S(1)}, u32[]{:S(2)}, u32[]{:S(2)}) collective-permute-start(bf16[4,32,16,128]{3,2,1,0:T(8,128)(2,1)S(1)} %get-tuple-element.13), channel_id=1, source_target_pairs={{0,1},{1,0},{2,3},{3,2},{4,5},{5,4},{6,7},{7,6},{8,9},{9,8},{10,11... | collective-permute-start | bytes 1572872 | tf_op jit(solution)/shard_map/ppermute | solution.py:456

commit v6 on v5

--- a/solution.py
+++ b/solution.py
@@ -312,7 +312,7 @@
 
 
 def y_kernel(occ_ref, in_ref, *refs):
-    weight_refs, (keep_ref, send_ref, hs) = refs[:5], refs[5:]
+    weight_refs, (keep_ref, send_low, send_high, hs) = refs[:5], refs[5:]
     core = lax.axis_index("core")
     held = hs.reshape(4, 16, 2, 4, Y_STRIDE, 128)
     for side in range(2):
@@ -333,14 +333,15 @@
         if u % 2:
             k = u // 2
             for p in range(32):
-                for ref, side in ((keep_ref, core), (send_ref, 1 - core)):
+                send_ref = send_low if k < 2 else send_high
+                for ref, at, side in ((keep_ref, k, core), (send_ref, k % 2, 1 - core)):
                     rows = [held[k, p // 2, p % 2, side * 2 + j, :8, :] for j in range(2)]
-                    ref[k, p] = jnp.concatenate(rows, axis=0).astype(BF16)
+                    ref[at, p] = jnp.concatenate(rows, axis=0).astype(BF16)
 
     staggered([attend_quad(load_quad(u), weights, masks[u // 2]) for u in range(8)], finish)
 
 
-def z_kernel(occ_ref, kept_ref, got_ref, *refs):
+def z_kernel(occ_ref, kept_ref, got_low, got_high, *refs):
     weight_refs, (out_ref, mask_ref) = refs[:5], refs[5:]
     first = lax.axis_index("core") == 0
     weights = Weights(2, *weight_refs)
@@ -359,8 +360,9 @@
                 for u in (quad * 2, quad * 2 + 1):
                     pair = ([], [])
                     for t in range(4):
-                        for ref in (kept_ref, got_ref):
-                            both = ref[t, u].astype(F32)
+                        got_ref = got_low if t < 2 else got_high
+                        for ref, at in ((kept_ref, t), (got_ref, t % 2)):
+                            both = ref[at, u].astype(F32)
                             pair[0].append(both[:8])
                             pair[1].append(both[8:])
                     lines.extend(jnp.concatenate(rows, axis=0) for rows in pair)
@@ -443,27 +445,28 @@
     planes = lax.all_to_all(after_x.reshape(128, 32, 128), every, 0, 0, tiled=True)
 
     half = jax.ShapeDtypeStruct((4, 32, 16, 128), BF16)
-    kept, sent = pl.pallas_call(
+    quarter = jax.ShapeDtypeStruct((2, 32, 16, 128), BF16)
+    kept, *sent = pl.pallas_call(
         y_kernel,
-        out_shape=(half, half),
+        out_shape=(half, quarter, quarter),
         in_specs=[VMEM] * 7,
-        out_specs=(VMEM, VMEM),
+        out_specs=(VMEM, VMEM, VMEM),
         scratch_shapes=[pltpu.VMEM((4 * 128 * Y_STRIDE, 128), F32)],
         compiler_params=PARAMS,
         name="y_phase",
     )(occupancy, planes.reshape(2, 64, 32, 128), *params)
 
-    got = lax.ppermute(sent, "core", [(0, 1), (1, 0)])
+    got = [lax.ppermute(part, "core", [(0, 1), (1, 0)]) for part in sent]
 
     after_z = pl.pallas_call(
         z_kernel,
         out_shape=jax.ShapeDtypeStruct((2, 64, 32, 128), BF16),
-        in_specs=[VMEM] * 8,
+        in_specs=[VMEM] * 9,
         out_specs=VMEM,
         scratch_shapes=[pltpu.VMEM((8, 64, 128), F32)],
         compiler_params=PARAMS,
         name="z_phase",
-    )(occupancy, kept, got, *params)
+    )(occupancy, kept, *got, *params)
 
     home = lax.all_to_all(after_z.reshape(128, 32, 128), every, 0, 0, tiled=True)
 

time: 79 us -> 78.8 us (level)
    ppermute x1 -> x2, starting transfers between devices: 1.51 us -> 1.6 us  [body(): got = [lax.ppermute(part, 'core', [(0, 1), (1, 0)]) for part in sent]]
  transfers between devices with their start and end apart: 1 -> 2, of which waited for: 1 -> 2; matrix products, arithmetic and copies ran while one was open for 0% -> 0% of each run, Pallas kernels for 0% -> 0%
where the time goes in v6:
time: 78.8 us; the launch traced here: 78.6 us
  blocking collectives  51.8 us (66%)
  Pallas kernels  23.6 us (30%)
  starting transfers between devices  1.6 us (2%)
  waiting for transfers between devices  1.22 us (2%)
    all_to_all x1, blocking collectives, body(): lax.all_to_all(after_x.reshape(128, 32, 128), every, 0, 0, tiled=True)  29.5 us
    all_to_all x1, blocking collectives, body(): lax.all_to_all(after_z.reshape(128, 32, 128), every, 0, 0, tiled=True)  22.4 us
    pallas_call x1, Pallas kernels, body(): pl.pallas_call(x_kernel, out_shape=(jax.ShapeDtypeStruct((2, 64, 32, 128)...  8.92 us
    pallas_call x1, Pallas kernels, body(): pl.pallas_call(y_kernel, out_shape=(half, quarter, quarter), in_specs=[VM...  7.71 us
    pallas_call x1, Pallas kernels, body(): pl.pallas_call(z_kernel, out_shape=jax.ShapeDtypeStruct((2, 64, 32, 128),...  5.91 us
    ppermute x2, starting transfers between devices, body(): got = [lax.ppermute(part, 'core', [(0, 1), (1, 0)]) for part in sent]  1.6 us
  transfers between devices with their start and end apart: 2, of which 2 were waited for; matrix products, arithmetic and copies ran while one was open for 0% of the time, Pallas kernels for 0%

profile of v6, /device:TPU:1, one launch (start us, length us, event | category | flops | bytes accessed | tf_op | source)
XLA Modules:
  0.0 78.6 jit_solution(9209338883229075778)
XLA Ops:
  0.0 0.0 copy-start.3
  0.0 0.0 copy-start.2
  0.0 0.0 copy-start.1
  0.0 0.0 copy-start
  0.0 0.0 copy-start.5
  0.0 0.0 copy-start.4
  0.0 8.9 %x_phase.1 = (bf16[2,64,32,128]{3,2,1,0:T(8,128)(2,1)}, bf16[256,4,16,128]{3,2,1,0:T(8,128)(2,1)}, s32[8,128]{1,0:T(8,128)}) custom-call(s32[8,4,16]{2,1,0:T(4,128)} %bitcast.8, bf16[256,4,16,128]{3,2,1,0:T(8,128)(2,1)} %vol_ref.1, f32[3,128]{1,0:T(4,128)} %refs_0_.5, bf16[3,128,128]{2,1,0:T(8,128)(2,1)} %refs_1_.5, bf16[3,128,128]{2,1,0:T(8,128)(2,1)} %refs_2_.5, ...), custom_call_target="tpu_custom_call" | custom-call | tf_op jit(solution)/shard_map/x_phase/pallas_call | solution.py:416
  9.0 0.0 copy-start.6
  9.0 29.5 %all_to_all.10 = bf16[128,32,128]{2,1,0:T(8,128)(2,1)S(1)} all-to-all(bf16[128,32,128]{2,1,0:T(8,128)(2,1)} %bitcast.11), channel_id=1, replica_groups=mesh['slab'=4,'chip'=16,'core'=2] {'core','slab','chip'}, dimensions={0} | all-to-all | bytes 2097152 | tf_op jit(solution)/shard_map/all_to_all | solution.py:445
  38.4 0.0 copy-done.3
  38.4 0.0 copy-done.2
  38.4 0.0 copy-done.1
  38.4 0.0 copy-done
  38.5 0.0 copy-done.5
  38.5 0.0 copy-done.4
  38.5 7.7 %y_phase.1 = (bf16[4,32,16,128]{3,2,1,0:T(8,128)(2,1)S(1)}, bf16[2,32,16,128]{3,2,1,0:T(8,128)(2,1)S(1)}, bf16[2,32,16,128]{3,2,1,0:T(8,128)(2,1)S(1)}) custom-call(s32[8,4,16]{2,1,0:T(4,128)S(1)} %bitcast.9, bf16[2,64,32,128]{3,2,1,0:T(8,128)(2,1)S(1)} %bitcast.6, f32[3,128]{1,0:T(4,128)S(1)} %copy-done.5, bf16[3,128,128]{2,1,0:T(8,128)(2,1)S(1)} %copy-done, ...), custom_call_target="tpu_custom_call" | custom-call | tf_op jit(solution)/shard_map/y_phase/pallas_call | solution.py:449
  46.2 1.3 %collective-permute-start = (bf16[2,32,16,128]{3,2,1,0:T(8,128)(2,1)S(1)}, bf16[2,32,16,128]{3,2,1,0:T(8,128)(2,1)S(1)}, u32[]{:S(2)}, u32[]{:S(2)}) collective-permute-start(bf16[2,32,16,128]{3,2,1,0:T(8,128)(2,1)S(1)} %get-tuple-element.14), channel_id=1, source_target_pairs={{0,1},{1,0},{2,3},{3,2},{4,5},{5,4},{6,7},{7,6},{8,9},{9,8},{10,11... | collective-permute-start | bytes 786440 | tf_op jit(solution)/shard_map/ppermute | solution.py:459
  47.5 0.3 collective-permute-start.1
  47.8 0.8 %collective-permute-done.got_low = bf16[2,32,16,128]{3,2,1,0:T(8,128)(2,1)S(1)} collective-permute-done((bf16[2,32,16,128]{3,2,1,0:T(8,128)(2,1)S(1)}, bf16[2,32,16,128]{3,2,1,0:T(8,128)(2,1)S(1)}, u32[]{:S(2)}, u32[]{:S(2)}) %collective-permute-start) | collective-permute-done | bytes 262176 | tf_op jit(solution)/shard_map/ppermute | solution.py:459
  48.6 0.4 collective-permute-done.1.got_high
  49.0 5.9 %z_phase.1 = bf16[2,64,32,128]{3,2,1,0:T(8,128)(2,1)S(1)} custom-call(s32[8,4,16]{2,1,0:T(4,128)S(1)} %bitcast.10, bf16[4,32,16,128]{3,2,1,0:T(8,128)(2,1)S(1)} %get-tuple-element.13.kept_ref, bf16[2,32,16,128]{3,2,1,0:T(8,128)(2,1)S(1)} %collective-permute-done.got_low, bf16[2,32,16,128]{3,2,1,0:T(8,128)(2,1)S(1)} %collective-permute-done.1.got_high, ...), custom_call_target="tpu_custom_call" | custom-call | tf_op jit(solution)/shard_map/z_phase/pallas_call | solution.py:461
  54.9 22.4 %all_to_all.11 = bf16[128,32,128]{2,1,0:T(8,128)(2,1)S(1)} all-to-all(bf16[128,32,128]{2,1,0:T(8,128)(2,1)S(1)} %bitcast.7), channel_id=1, replica_groups=mesh['slab'=4,'chip'=16,'core'=2] {'core','slab','chip'}, dimensions={0} | all-to-all | bytes 2097152 | tf_op jit(solution)/shard_map/all_to_all | solution.py:471
  77.3 0.0 copy-done.6
  77.3 1.1 %merge.1 = bf16[256,4,16,128]{3,2,1,0:T(8,128)(2,1)} custom-call(s32[8,128]{1,0:T(8,128)S(1)} %copy-done.6, bf16[2,64,2,16,128]{4,3,2,1,0:T(8,128)(2,1)S(1)} %bitcast.5, bf16[256,4,16,128]{3,2,1,0:T(8,128)(2,1)} %get-tuple-element.16.res_in_ref), custom_call_target="tpu_custom_call", output_to_operand_aliasing={{}: (2, {})} | custom-call | tf_op jit(solution)/shard_map/merge/pallas_call | solution.py:473
Async XLA Ops:
  0.0 38.4 %copy-start.3 = (bf16[3,128,128]{2,1,0:T(8,128)(2,1)S(1)}, bf16[3,128,128]{2,1,0:T(8,128)(2,1)}, u32[]{:S(2)}) copy-start(bf16[3,128,128]{2,1,0:T(8,128)(2,1)} %refs_4_.5) | copy-start | bytes 294916
  0.0 38.4 %copy-start.2 = (bf16[3,128,128]{2,1,0:T(8,128)(2,1)S(1)}, bf16[3,128,128]{2,1,0:T(8,128)(2,1)}, u32[]{:S(2)}) copy-start(bf16[3,128,128]{2,1,0:T(8,128)(2,1)} %refs_3_.5) | copy-start | bytes 294916
  0.0 38.4 %copy-start.1 = (bf16[3,128,128]{2,1,0:T(8,128)(2,1)S(1)}, bf16[3,128,128]{2,1,0:T(8,128)(2,1)}, u32[]{:S(2)}) copy-start(bf16[3,128,128]{2,1,0:T(8,128)(2,1)} %refs_2_.5) | copy-start | bytes 294916
  0.0 38.4 %copy-start = (bf16[3,128,128]{2,1,0:T(8,128)(2,1)S(1)}, bf16[3,128,128]{2,1,0:T(8,128)(2,1)}, u32[]{:S(2)}) copy-start(bf16[3,128,128]{2,1,0:T(8,128)(2,1)} %refs_1_.5) | copy-start | bytes 294916
  0.0 38.4 %copy-start.5 = (f32[3,128]{1,0:T(4,128)S(1)}, f32[3,128]{1,0:T(4,128)}, u32[]{:S(2)}) copy-start(f32[3,128]{1,0:T(4,128)} %refs_0_.5) | copy-start | bytes 4612
  0.0 38.4 %copy-start.4 = (s32[16,8,4]{0,2,1:T(4,128)S(1)}, s32[16,8,4]{0,2,1:T(4,128)}, u32[]{:S(2)}) copy-start(s32[16,8,4]{0,2,1:T(4,128)} %param.8) | copy-start | bytes 6148
  9.0 68.4 %copy-start.6 = (s32[8,128]{1,0:T(8,128)S(1)}, s32[8,128]{1,0:T(8,128)}, u32[]{:S(2)}) copy-start(s32[8,128]{1,0:T(8,128)} %get-tuple-element.11.starts_ref) | copy-start | bytes 12292
  46.2 2.5 %collective-permute-start = (bf16[2,32,16,128]{3,2,1,0:T(8,128)(2,1)S(1)}, bf16[2,32,16,128]{3,2,1,0:T(8,128)(2,1)S(1)}, u32[]{:S(2)}, u32[]{:S(2)}) collective-permute-start(bf16[2,32,16,128]{3,2,1,0:T(8,128)(2,1)S(1)} %get-tuple-element.14), channel_id=1, source_target_pairs={{0,1},{1,0},{2,3},{3,2},{4,5},{5,4},{6,7},{7,6},{8,9},{9,8},{10,11... | collective-permute-start | bytes 786440 | tf_op jit(solution)/shard_map/ppermute | solution.py:459
  47.5 1.5 %collective-permute-start.1 = (bf16[2,32,16,128]{3,2,1,0:T(8,128)(2,1)S(1)}, bf16[2,32,16,128]{3,2,1,0:T(8,128)(2,1)S(1)}, u32[]{:S(2)}, u32[]{:S(2)}) collective-permute-start(bf16[2,32,16,128]{3,2,1,0:T(8,128)(2,1)S(1)} %get-tuple-element.15), channel_id=1, source_target_pairs={{0,1},{1,0},{2,3},{3,2},{4,5},{5,4},{6,7},{7,6},{8,9},{9,8},{10,11... | collective-permute-start | bytes 786440 | tf_op jit(solution)/shard_map/ppermute | solution.py:459
